TPU v7x, 32 devices: a whole 2x2x4 slice. The times are simulated.
32 devices in a mesh: rows: 8 (over z, x), seq: 4 (over y, core).
Axes of the slice: x: 2, y: 2, z: 4, core: 2. Of those that a mesh axis runs over, the one named last changes fastest.
Arguments:
- layer_input: bfloat16 [32, 576, 768], P('rows', 'seq'), may hold values from -6 to 6
- first_gain: bfloat16 [768], replicated, may hold values from 0.25 to 1.75
- first_shift: bfloat16 [768], replicated, may hold values from -4 to 4
- input_weight: bfloat16 [768, 2304], replicated, may hold values from -0.21875 to 0.21875
- query_bias: bfloat16 [768], replicated, may hold values from -4 to 4
- value_bias: bfloat16 [768], replicated, may hold values from -4 to 4
- bias_table: bfloat16 [2209, 12], replicated, may hold values from -4 to 4
- output_weight: bfloat16 [768, 768], replicated, may hold values from -0.875 to 0.875
- output_bias: bfloat16 [768], replicated, may hold values from -4 to 4
- attention_scale: bfloat16 [768], replicated, may hold values from 0.5 to 2
- second_gain: bfloat16 [768], replicated, may hold values from 0.25 to 1.75
- second_shift: bfloat16 [768], replicated, may hold values from -4 to 4
- up_weight: bfloat16 [768, 3072], replicated, may hold values from -0.21875 to 0.21875
- up_bias: bfloat16 [3072], replicated, may hold values from -4 to 4
- down_weight: bfloat16 [3072, 768], replicated, may hold values from -0.21875 to 0.21875
- down_bias: bfloat16 [768], replicated, may hold values from -4 to 4
- feed_scale: bfloat16 [768], replicated, may hold values from 0.5 to 2
- upstream: bfloat16 [32, 576, 768], P('rows', 'seq'), may hold values from -6 to 6
- grid_heights: int32 [32, 4], P('rows'), may hold values from 1 to 23, as said below
- grid_widths: int32 [32, 4], P('rows'), may hold values from 1 to 23, as said below
- packing_order: int32 [32, 4], P('rows'), may hold values from 0 to 3, each once within a row
Outputs:
- layer_output: bfloat16 [32, 576, 768], P('rows', 'seq')
- input_gradient: float32 [32, 576, 768], P('rows', 'seq')
- first_gain_gradient: float32 [768], replicated
- first_shift_gradient: float32 [768], replicated
- input_weight_gradient: float32 [768, 2304], P('rows', 'seq')
- query_bias_gradient: float32 [768], replicated
- value_bias_gradient: float32 [768], replicated
- bias_table_gradient: float32 [2209, 12], replicated
- output_weight_gradient: float32 [768, 768], P('rows', 'seq')
- output_bias_gradient: float32 [768], replicated
- attention_scale_gradient: float32 [768], replicated
- second_gain_gradient: float32 [768], replicated
- second_shift_gradient: float32 [768], replicated
- up_weight_gradient: float32 [768, 3072], P('rows', 'seq')
- up_bias_gradient: float32 [3072], replicated
- down_weight_gradient: float32 [3072, 768], P('rows', 'seq')
- down_bias_gradient: float32 [768], replicated
- feed_scale_gradient: float32 [768], replicated
Inputs may be any that keep to these rules, and one draw needn't show every extreme that they name: `grid_heights`: column 0 of each packed row is its large image, with height and width at least 21; the other images have sides of at most 3; a row's images together fill at most 576 slots. `grid_widths`: as for grid_heights, column by column.
All inputs are finite; a program needn't handle non-finite values.
Results may differ from a plain program's by a relative error of at most 0.019.
Values may be sent and summed in bfloat16 or wider, within the bound.
A program may use at most 384 MiB of HBM per device.

v0:
```python
from functools import partial

import jax
import jax.numpy as jnp
from jax import lax
from jax.sharding import PartitionSpec as P

HEADS = 12
HEAD = 64
GRID = 24
SLOTS = 576


EPS = 1e-06
NEGATIVE = -1e30
HIGHEST = lax.Precision.HIGHEST


def shifted(value, axis, steps):
    count = lax.axis_size(axis)
    pairs = [(source, (source + steps) % count) for source in range(count)]
    return lax.ppermute(value, axis, pairs)


def arrange(heights, widths, order, count):
    images = heights.shape[-1]
    numbers = jnp.arange(images, dtype=jnp.int32)
    picked = order[:, :, None] == numbers[None, None, :]
    sizes = jnp.sum(jnp.where(picked, (heights * widths)[:, None, :], 0), -1)
    breadth = jnp.sum(jnp.where(picked, widths[:, None, :], 0), -1)
    finish = jnp.cumsum(sizes, -1)
    begin = finish - sizes
    places = jnp.arange(count, dtype=jnp.int32)[None, :, None]
    inside = (places >= begin[:, None, :]) & (places < finish[:, None, :])
    offset = places - begin[:, None, :]
    across = breadth[:, None, :]
    segment = jnp.where(jnp.any(inside, -1), jnp.sum(jnp.where(inside, numbers, 0), -1), images)
    row_number = jnp.sum(jnp.where(inside, offset // across, 0), -1)
    column_number = jnp.sum(jnp.where(inside, offset % across, 0), -1)
    return (segment, row_number, column_number)


def normalize(values, gain, shift):
    center = values - jnp.mean(values, -1, keepdims=True)
    spread = lax.rsqrt(jnp.mean(center * center, -1, keepdims=True) + EPS)
    normal = center * spread
    return (normal * gain + shift, normal, spread)


def normalize_back(change, normal, spread, gain):
    scaled = change * gain
    inner = (
        scaled
        - jnp.mean(scaled, -1, keepdims=True)
        - normal * jnp.mean(scaled * normal, -1, keepdims=True)
    )
    return inner * spread


def product(left, right, form):
    return jnp.einsum(form, left, right, preferred_element_type=jnp.float32)


def selectors(query_place):
    sides = jnp.arange(GRID, dtype=jnp.int32)
    spans = jnp.arange(2 * GRID - 1, dtype=jnp.int32)
    row_pick = (
        query_place[1].reshape(-1)[:, None, None] - sides[None, :, None] + GRID - 1
        == spans[None, None, :]
    )
    column_pick = (
        query_place[2].reshape(-1)[:, None, None] - sides[None, :, None] + GRID - 1
        == spans[None, None, :]
    )
    return (row_pick, column_pick)


def on_device(
    layer_input,
    first_gain,
    first_shift,
    input_weight,
    query_bias,
    value_bias,
    bias_table,
    output_weight,
    output_bias,
    attention_scale,
    second_gain,
    second_shift,
    up_weight,
    up_bias,
    down_weight,
    down_bias,
    feed_scale,
    upstream,
    grid_heights,
    grid_widths,
    packing_order,
):
    parts = lax.axis_size("seq")
    shard_index = lax.axis_index("seq")
    factor = HEAD ** (-0.5)
    places = arrange(grid_heights, grid_widths, packing_order, SLOTS)
    local_input, local_upstream = (layer_input, upstream)
    query_place = tuple(
        (
            lax.dynamic_slice_in_dim(
                item, shard_index * layer_input.shape[1], layer_input.shape[1], 1
            )
            for item in places
        )
    )
    rows, width_slots, model = local_input.shape
    tokens = local_input.reshape(-1, model).astype(jnp.float32)
    row_pick, column_pick = selectors(query_place)
    table_grid = bias_table.reshape(2 * GRID - 1, 2 * GRID - 1, HEADS)
    row_slab = product(row_pick.astype(jnp.bfloat16), table_grid, "nra,abh->nrbh").astype(
        jnp.bfloat16
    )
    window = product(row_slab, column_pick.astype(jnp.bfloat16), "nrbh,ncb->nrch").astype(
        jnp.bfloat16
    )
    window = window.reshape(rows, width_slots, GRID * GRID, HEADS)
    cell_ids = jnp.arange(GRID * GRID, dtype=jnp.int32)
    first_in, first_normal, first_spread = normalize(tokens, first_gain, first_shift)
    first_low = first_in.astype(jnp.bfloat16)
    mixed = product(first_low, input_weight, "nd,de->ne")
    shape_heads = (rows, width_slots, HEADS, HEAD)
    query = ((mixed[:, :model] + query_bias) * factor).astype(jnp.bfloat16).reshape(shape_heads)
    keys = mixed[:, model : 2 * model].astype(jnp.bfloat16).reshape(shape_heads)
    values = (mixed[:, 2 * model :] + value_bias).astype(jnp.bfloat16).reshape(shape_heads)
    pair = jnp.stack([keys, values])

    def block_terms(key_block, start):
        count = key_block.shape[1]
        key_place = tuple((lax.dynamic_slice_in_dim(item, start, count, 1) for item in places))
        same = query_place[0][:, :, None] == key_place[0][:, None, :]
        key_cell = key_place[1] * GRID + key_place[2]
        key_pick = (key_cell[:, :, None] == cell_ids[None, None, :]).astype(jnp.bfloat16)
        score = product(query, key_block, "rqhd,rkhd->hrqk") + product(
            window, key_pick, "rqph,rkp->hrqk"
        )
        return (jnp.where(same[None], score, NEGATIVE), key_pick)

    start_state = (
        jnp.full((HEADS, rows, width_slots), NEGATIVE, jnp.float32),
        jnp.zeros((HEADS, rows, width_slots), jnp.float32),
        jnp.zeros(shape_heads, jnp.float32),
    )
    state = start_state
    moving = pair
    for turn in range(parts):
        source = (shard_index - turn) % parts
        attend_top, attend_total, attend_summed = state
        attend_score, attend_key_pick = block_terms(moving[0], source * width_slots)
        new_top = jnp.maximum(attend_top, jnp.max(attend_score, -1))
        decay = jnp.exp(attend_top - new_top)
        weight = jnp.exp(attend_score - new_top[..., None])
        attend_total = attend_total * decay + jnp.sum(weight, -1)
        attend_summed = attend_summed * jnp.transpose(decay, (1, 2, 0))[..., None] + product(
            weight.astype(jnp.bfloat16), moving[1], "hrqk,rkhd->rqhd"
        )
        state = (new_top, attend_total, attend_summed)
        if turn + 1 < parts:
            moving = shifted(moving, "seq", 1)
    top, total, summed = state
    log_total = top + jnp.log(total)
    attended = (summed / jnp.transpose(total, (1, 2, 0))[..., None]).reshape(-1, model)
    attended_low = attended.astype(jnp.bfloat16)
    branch = product(attended_low, output_weight, "nd,de->ne") + output_bias
    middle = tokens + attention_scale * branch
    second_in, second_normal, second_spread = normalize(middle, second_gain, second_shift)
    second_low = second_in.astype(jnp.bfloat16)
    hidden = product(second_low, up_weight, "nd,df->nf") + up_bias
    active, gelu_pull = jax.vjp(partial(jax.nn.gelu, approximate=False), hidden)
    active_low = active.astype(jnp.bfloat16)
    outcome = product(active_low, down_weight, "nf,fd->nd") + down_bias
    local_output = (middle + feed_scale * outcome).astype(jnp.bfloat16).reshape(local_input.shape)
    change = local_upstream.reshape(-1, model).astype(jnp.float32)
    feed_scale_gradient = jnp.sum(change * outcome, 0)
    outcome_change = (change * feed_scale).astype(jnp.bfloat16)
    down_bias_gradient = jnp.sum(outcome_change.astype(jnp.float32), 0)
    down_weight_gradient = product(active_low, outcome_change, "nf,nd->fd")
    (hidden_change,) = gelu_pull(product(outcome_change, down_weight, "nd,fd->nf"))
    hidden_low = hidden_change.astype(jnp.bfloat16)
    up_bias_gradient = jnp.sum(hidden_low.astype(jnp.float32), 0)
    up_weight_gradient = product(second_low, hidden_low, "nd,nf->df")
    second_change = product(hidden_low, up_weight, "nf,df->nd")
    second_gain_gradient = jnp.sum(second_change * second_normal, 0)
    second_shift_gradient = jnp.sum(second_change, 0)
    middle_change = change + normalize_back(
        second_change, second_normal, second_spread, second_gain
    )
    attention_scale_gradient = jnp.sum(middle_change * branch, 0)
    branch_change = (middle_change * attention_scale).astype(jnp.bfloat16)
    output_bias_gradient = jnp.sum(branch_change.astype(jnp.float32), 0)
    output_weight_gradient = product(attended_low, branch_change, "nd,ne->de")
    attended_change = product(branch_change, output_weight, "ne,de->nd").astype(jnp.bfloat16)
    delta = jnp.transpose(
        jnp.sum((attended_change.astype(jnp.float32) * attended).reshape(shape_heads), -1),
        (2, 0, 1),
    )
    change_heads = attended_change.reshape(shape_heads)

    def attend_back(pieces, start):
        score, key_pick = block_terms(pieces[0], start)
        chance = jnp.exp(score - log_total[..., None])
        weight_change = product(change_heads, pieces[1], "rqhd,rkhd->hrqk")
        score_change = (chance * (weight_change - delta[..., None])).astype(jnp.bfloat16)
        query_term = product(score_change, pieces[0], "hrqk,rkhd->rqhd")
        key_term = product(score_change, query, "hrqk,rqhd->rkhd")
        value_term = product(chance.astype(jnp.bfloat16), change_heads, "hrqk,rqhd->rkhd")
        window_term = product(score_change, key_pick, "hrqk,rkp->rqph")
        return (query_term, jnp.stack([key_term, value_term]), window_term)

    moving = pair
    carried = jnp.zeros((2,) + shape_heads, jnp.float32)
    query_sum = jnp.zeros(shape_heads, jnp.float32)
    window_sum = jnp.zeros(window.shape, jnp.float32)
    for turn in range(parts):
        source = (shard_index - turn) % parts
        query_term, pair_term, window_term = attend_back(moving, source * width_slots)
        query_sum = query_sum + query_term
        window_sum = window_sum + window_term
        carried = carried + pair_term
        if turn + 1 < parts:
            moving = shifted(moving, "seq", 1)
            carried = shifted(carried.astype(jnp.bfloat16), "seq", 1).astype(carried.dtype)
    carried = shifted(carried.astype(jnp.bfloat16), "seq", 1).astype(carried.dtype)
    window_grid = window_sum.reshape(rows * width_slots, GRID, GRID, HEADS)
    slab_change = jnp.einsum(
        "nrch,ncb->nrbh", window_grid, column_pick.astype(jnp.float32), precision=HIGHEST
    )
    table_gradient = jnp.einsum(
        "nra,nrbh->abh", row_pick.astype(jnp.float32), slab_change, precision=HIGHEST
    ).reshape(-1, HEADS)
    query_low = (query_sum.astype(jnp.bfloat16) * factor).reshape(-1, model)
    key_low = carried[0].astype(jnp.bfloat16).reshape(-1, model)
    value_low = carried[1].astype(jnp.bfloat16).reshape(-1, model)
    joined = jnp.concatenate([query_low, key_low, value_low], axis=1)
    query_bias_gradient = jnp.sum(query_low.astype(jnp.float32), 0)
    value_bias_gradient = jnp.sum(value_low.astype(jnp.float32), 0)
    input_weight_gradient = product(first_low, joined, "nd,ne->de")
    first_change = product(joined, input_weight, "ne,de->nd")
    first_gain_gradient = jnp.sum(first_change * first_normal, 0)
    first_shift_gradient = jnp.sum(first_change, 0)
    local_gradient = (
        middle_change + normalize_back(first_change, first_normal, first_spread, first_gain)
    ).reshape(local_input.shape)
    weights_local = (
        input_weight_gradient,
        output_weight_gradient,
        up_weight_gradient,
        down_weight_gradient,
    )
    partial_sums = (
        lax.psum_scatter(weights_local[0], "rows", scatter_dimension=0, tiled=True),
        lax.psum_scatter(weights_local[1], "rows", scatter_dimension=0, tiled=True),
        lax.psum_scatter(weights_local[2], "rows", scatter_dimension=0, tiled=True),
        lax.psum_scatter(weights_local[3], "rows", scatter_dimension=0, tiled=True),
    )
    weights_done = (
        lax.psum_scatter(
            partial_sums[0].astype(jnp.bfloat16), "seq", scatter_dimension=1, tiled=True
        ).astype(jnp.float32),
        lax.psum_scatter(
            partial_sums[1].astype(jnp.bfloat16), "seq", scatter_dimension=1, tiled=True
        ).astype(jnp.float32),
        lax.psum_scatter(
            partial_sums[2].astype(jnp.bfloat16), "seq", scatter_dimension=1, tiled=True
        ).astype(jnp.float32),
        lax.psum_scatter(
            partial_sums[3].astype(jnp.bfloat16), "seq", scatter_dimension=1, tiled=True
        ).astype(jnp.float32),
    )
    small_done = lax.psum(
        (
            first_gain_gradient,
            first_shift_gradient,
            query_bias_gradient,
            value_bias_gradient,
            table_gradient,
            output_bias_gradient,
            attention_scale_gradient,
            second_gain_gradient,
            second_shift_gradient,
            up_bias_gradient,
            down_bias_gradient,
            feed_scale_gradient,
        ),
        ("rows", "seq"),
    )
    return (
        local_output,
        local_gradient,
        small_done[0],
        small_done[1],
        weights_done[0],
        small_done[2],
        small_done[3],
        small_done[4],
        weights_done[1],
        small_done[5],
        small_done[6],
        small_done[7],
        small_done[8],
        weights_done[2],
        small_done[9],
        weights_done[3],
        small_done[10],
        small_done[11],
    )


def solution(mesh):
    in_specs = (
        P("rows", "seq", None),
        P(),
        P(),
        P(),
        P(),
        P(),
        P(),
        P(),
        P(),
        P(),
        P(),
        P(),
        P(),
        P(),
        P(),
        P(),
        P(),
        P("rows", "seq", None),
        P("rows", None),
        P("rows", None),
        P("rows", None),
    )
    out_specs = (
        P("rows", "seq", None),
        P("rows", "seq", None),
        P(),
        P(),
        P("rows", "seq"),
        P(),
        P(),
        P(),
        P("rows", "seq"),
        P(),
        P(),
        P(),
        P(),
        P("rows", "seq"),
        P(),
        P("rows", "seq"),
        P(),
        P(),
    )
    return jax.shard_map(
        on_device, mesh=mesh, in_specs=in_specs, out_specs=out_specs, check_vma=False
    )
```

profile of v0, /device:TPU:8, one launch (start us, length us, event | category | flops | bytes accessed | tf_op | source)
XLA Modules:
  0.0 1291.3 jit_solution(10761407055354990398)
XLA Ops:
  23.9 4.0 reshape.342
  27.9 4.4 copy.279
  35.8 4.0 reshape.343
  39.8 4.4 copy.280
  44.2 4.2 pad_maximum_fusion
  69.5 4.5 reshape.321
  74.0 4.5 squeeze_stack_reshape.4
  78.5 9.6 convolution_convert_fusion
  88.1 71.9 %copy.270 = bf16[576,24,47,12]{2,1,3,0:T(8,128)(2,1)} copy(bf16[576,24,47,12]{0,2,3,1:T(8,128)(2,1)} %convolution_convert_fusion) | data formatting | bytes 31186944 | tf_op jit(solution)/shard_map/convert_element_type | solution.py:118
  159.9 76.6 %convert_bitcast_fusion = bf16[576,24,24,12]{1,2,3,0:T(8,128)(2,1)} fusion(bf16[576,24,47,12]{2,1,3,0:T(8,128)(2,1)} %copy.270, s32[576,24]{1,0:T(8,128)} %copy.268), kind=kOutput, calls=%fused_computation.2 | convolution fusion | flops 378874368 | bytes 23611392 | tf_op jit(solution)/shard_map/nrbh,ncb->nrch/dot_general | solution.py:61
  236.5 43.1 %copy.271 = bf16[576,24,24,12]{0,2,1,3:T(8,128)(2,1)} copy(bf16[576,24,24,12]{1,2,3,0:T(8,128)(2,1)} %convert_bitcast_fusion) | data formatting | bytes 15925248 | tf_op jit(solution)/shard_map/convert_element_type | solution.py:121
  279.6 27.4 %reshape.323 = bf16[4,144,576,12]{1,0,2,3:T(4,128)(2,1)} reshape(bf16[576,24,24,12]{0,2,1,3:T(8,128)(2,1)} %copy.271) | data formatting | bytes 15925248 | tf_op jit(solution)/shard_map/reshape | solution.py:124
  307.0 23.3 %copy.272 = bf16[4,144,576,12]{2,1,0,3:T(8,128)(2,1)} copy(bf16[4,144,576,12]{1,0,2,3:T(4,128)(2,1)} %reshape.323) | data formatting | bytes 15925248 | tf_op jit(solution)/shard_map/reshape | solution.py:124
  332.5 6.1 fusion.122
  338.7 5.8 fusion.148
  344.5 5.9 fusion.145
  362.0 4.5 squeeze_stack_reshape.10
  366.6 9.6 fusion.142
  376.2 9.1 fusion.219
  387.7 4.0 slice_bitcast_fusion.5
  391.7 8.4 fusion.218
  400.1 4.0 slice_bitcast_fusion.3
  407.7 16.9 %collective-permute-done.2 = bf16[2,4,144,12,64]{2,4,1,3,0:T(8,128)(2,1)S(1)} collective-permute-done((bf16[2,4,144,12,64]{2,4,1,3,0:T(8,128)(2,1)}, bf16[2,4,144,12,64]{2,4,1,3,0:T(8,128)(2,1)S(1)}, u32[]{:S(2)}, u32[]{:S(2)}) %collective-permute-start.2) | collective-permute-done | bytes 1769504 | tf_op jit(solution)/shard_map/ppermute | solution.py:22
  424.6 6.1 fusion.216
  430.8 9.3 fusion.18
  440.1 4.8 fusion.22
  459.0 4.5 reshape.324
  463.6 4.8 multiply_add_fusion.1
  471.9 5.8 fusion.210
  477.7 22.5 %convert_reduce_fusion = (f32[3072]{0:T(1024)}, bf16[576,3072]{1,0:T(8,128)(2,1)}, f32[576,3072]{1,0:T(8,128)}) fusion(f32[576,3072]{1,0:T(8,128)S(1)} %fusion.210, f32[3072]{0:T(1024)S(1)} %copy-done.63, bf16[576,768]{1,0:T(8,128)(2,1)S(1)} %copy-done.42, bf16[3072,768]{1,0:T(8,128)(2,1)} %param.35), kind=kOutput, calls=%fused_computation.16 | convolution fusion | flops 2850616320 | bytes 23322624 | tf_op jit(solution)/shard_map/nd,fd->nf/dot_general | solution.py:61
  500.3 6.7 multiply_convert_fusion.4
  507.0 7.5 multiply_reduce_fusion
  514.6 5.0 fusion.104
  525.4 9.6 fusion.222
  535.1 10.2 fusion.209
  548.7 4.5 convert_multiply_fusion.1
  558.2 4.5 reshape.326
  562.7 4.7 reshape.327
  571.5 15.2 %fusion.26 = (bf16[12,4,144,144]{2,3,1,0:T(8,128)(2,1)S(1)}, bf16[12,4,144,144]{2,3,1,0:T(8,128)(2,1)}, bf16[12,4,144,144]{2,3,1,0:T(8,128)(2,1)}, bf16[12,4,144,144]{2,3,1,0:T(8,128)(2,1)}) fusion(f32[12,4,144,144]{2,3,1,0:T(8,128)} %get-tuple-element.180, f32[12,4,144]{2,1,0:T(4,128)S(1)} %log_add_fusion, f32[12,4,144,144]{2,3,1,0:T(8,128)} %get-tuple-element.178, ...), kind=kLoop, calls=%fused_computation.60 | loop fusion | flops 7962624 | bytes 23915520 | tf_op jit(solution)/shard_map/convert_element_type | solution.py:213
  588.1 4.2 multiply_convert_fusion.3
  606.1 27.1 %collective-permute-done.3 = bf16[2,4,144,12,64]{2,4,3,1,0:T(8,128)(2,1)} collective-permute-done((bf16[2,4,144,12,64]{2,4,3,1,0:T(8,128)(2,1)}, bf16[2,4,144,12,64]{2,4,3,1,0:T(8,128)(2,1)}, u32[]{:S(2)}, u32[]{:S(2)}) %collective-permute-start.3) | collective-permute-done | bytes 1769504 | tf_op jit(solution)/shard_map/ppermute | solution.py:22
  633.2 6.8 fusion.15
  649.8 27.2 %collective-permute-done.4 = bf16[2,4,144,12,64]{2,4,3,1,0:T(8,128)(2,1)} collective-permute-done((bf16[2,4,144,12,64]{2,4,3,1,0:T(8,128)(2,1)}, bf16[2,4,144,12,64]{2,4,3,1,0:T(8,128)(2,1)}, u32[]{:S(2)}, u32[]{:S(2)}) %collective-permute-start.4) | collective-permute-done | bytes 1769504 | tf_op jit(solution)/shard_map/ppermute | solution.py:22
  677.0 7.0 fusion.16
  691.9 29.3 %collective-permute-done.5 = bf16[2,4,144,12,64]{2,4,3,1,0:T(8,128)(2,1)} collective-permute-done((bf16[2,4,144,12,64]{2,4,3,1,0:T(8,128)(2,1)}, bf16[2,4,144,12,64]{2,4,3,1,0:T(8,128)(2,1)}, u32[]{:S(2)}, u32[]{:S(2)}) %collective-permute-start.5) | collective-permute-done | bytes 1769504 | tf_op jit(solution)/shard_map/ppermute | solution.py:22
  721.2 4.9 fusion.17
  735.8 4.3 reshape.328
  742.3 20.8 %collective-permute-done.6 = bf16[2,4,144,12,64]{2,4,3,1,0:T(8,128)(2,1)} collective-permute-done((bf16[2,4,144,12,64]{2,4,3,1,0:T(8,128)(2,1)}, bf16[2,4,144,12,64]{2,4,3,1,0:T(8,128)(2,1)}, u32[]{:S(2)}, u32[]{:S(2)}) %collective-permute-start.6) | collective-permute-done | bytes 1769504 | tf_op jit(solution)/shard_map/ppermute | solution.py:22
  768.9 3.9 convert_element_type.284
  772.8 3.8 copy.335
  776.6 3.9 convert_element_type.283
  785.1 6.9 fusion.221
  794.6 11.4 fusion.67
  806.0 8.1 fusion.61
  817.6 11.1 fusion.73
  833.1 28.8 %add_bitcast_fusion = f32[4,144,576,12]{2,1,3,0:T(8,128)} fusion(f32[4,576,12,144]{1,3,2,0:T(8,128)} %fusion.61, f32[4,576,12,144]{1,3,2,0:T(8,128)} %fusion.73, f32[4,576,12,144]{1,3,2,0:T(8,128)} %fusion.67, bf16[12,4,144,144]{2,3,1,0:T(8,128)(2,1)} %copy-done.8, s32[4,144]{1,0:T(4,128)S(1)} %copy-done.56), kind=kOutput, calls=%fused_computation.4 | convolution fusion | flops 1158893568 | bytes 65693952 | tf_op jit(solution)/shard_map/hrqk,rkp->rqph/dot_general | solution.py:61
  862.0 19.8 %copy.402 = f32[4,144,576,12]{2,3,1,0:T(8,128)} copy(f32[4,144,576,12]{2,1,3,0:T(8,128)} %add_bitcast_fusion) | data formatting | bytes 31850496 | tf_op jit(solution)/shard_map/reshape | solution.py:231
  881.7 55.7 %reshape.344 = f32[576,24,24,12]{2,1,3,0:T(8,128)} reshape(f32[4,144,576,12]{2,3,1,0:T(8,128)} %copy.402) | data formatting | bytes 31850496 | tf_op jit(solution)/shard_map/reshape | solution.py:231
  939.7 73.6 %convolution_bitcast_fusion = f32[576,24,47,12]{2,1,3,0:T(8,128)} fusion(f32[576,24,24,12]{2,1,3,0:T(8,128)} %reshape.344, s32[576,24]{1,0:T(8,128)} %copy.268), kind=kOutput, calls=%fused_computation.3 | convolution fusion | flops 2246109696 | bytes 47167488 | tf_op jit(solution)/shard_map/nrch,ncb->nrbh/dot_general | solution.py:232
  1013.3 44.9 %reduce-scatter.15.cloned.1.call-done = f32[96,2304]{1,0:T(8,128)} async-done(((f32[768,2304]{1,0:T(8,128)}), f32[96,2304]{1,0:T(8,128)}) %reduce-scatter.15.cloned.1.call-update) | async-done | bytes 884752 | tf_op jit(solution)/shard_map/reduce_scatter | solution.py:258
  1062.4 92.6 %fusion.155 = f32[47,47,12]{1,0,2:T(8,128)} fusion(f32[576,24,47,12]{2,1,3,0:T(8,128)} %convolution_bitcast_fusion, s32[576,24]{0,1:T(8,128)} %subtract_add_fusion), kind=kOutput, calls=%fused_computation.200 | convolution fusion | flops 4398008832 | bytes 31348272 | tf_op jit(solution)/shard_map/nra,nrbh->abh/dot_general | solution.py:235
  1161.1 6.3 multiply_reduce_fusion.2
  1171.1 41.9 %all-reduce = (f32[768]{0:T(1024)}, f32[768]{0:T(1024)}, f32[768]{0:T(1024)}, f32[768]{0:T(1024)}, f32[768]{0:T(1024)}, /*index=5*/f32[768]{0:T(1024)}, f32[768]...) all-reduce(f32[768]{0:T(1024)} %get-tuple-element.92, ...), channel_id=1, replica_groups=mesh['rows'=8,'seq'=4] {'rows','seq'}, use_global_device_ids=true, to_apply=%region_25.26 | all-reduce | flops 10752 | bytes 86016 | tf_op jit(solution)/shard_map/psum | solution.py:277
  1221.4 60.4 %all-reduce.3.cloned.1.call-done = f32[2209,12]{0,1:T(8,128)} async-done(((f32[2209,12]{0,1:T(8,128)}), f32[2209,12]{0,1:T(8,128)}) %all-reduce.3.cloned.1.call-update) | async-done | bytes 106048 | tf_op jit(solution)/shard_map/psum | solution.py:277
  (364 shorter events, 187.6 us)
Async XLA Ops:
  8.0 10.1 copy-start
  8.0 806.1 %reduce-scatter.17.cloned.1.call-start = ((), (), s32[]{:S(2)}) async-start(), calls=%async_computation.10 | async-start | bytes 2654208 | tf_op jit(solution)/shard_map/reduce_scatter | solution.py:259
  9.7 10.7 copy-start.69
  12.0 8.4 copy-start.71
  23.8 8.5 copy-start.83
  23.8 8.5 copy-start.84
  48.4 302.0 %collective-permute-start = (bf16[2,4,144,12,64]{2,4,1,3,0:T(8,128)(2,1)}, bf16[2,4,144,12,64]{2,4,1,3,0:T(8,128)(2,1)}, u32[]{:S(2)}, u32[]{:S(2)}) collective-permute-start(bf16[2,4,144,12,64]{2,4,1,3,0:T(8,128)(2,1)} %pad_maximum_fusion), channel_id=1, source_target_pairs={{0,1},{1,2},{2,3},{3,0},{4,5},{5,6},{6,7},{7,4},{8,9},{9,10},{10,1... | collective-permute-start | bytes 5308424 | tf_op jit(solution)/shard_map/ppermute | solution.py:22
  53.9 276.4 %copy-start.64 = (f32[768]{0:T(1024)}, f32[768]{0:T(1024)S(1)}, u32[]{:S(2)}) copy-start(f32[768]{0:T(1024)S(1)} %convert_element_type.252) | copy-start | bytes 9220
  58.5 280.2 %copy-start.55 = (s32[4,144]{1,0:T(4,128)}, s32[4,144]{1,0:T(4,128)S(1)}, u32[]{:S(2)}) copy-start(s32[4,144]{1,0:T(4,128)S(1)} %get-tuple-element.157) | copy-start | bytes 6916
  58.5 286.0 %copy-start.59 = (s32[4,144]{1,0:T(4,128)}, s32[4,144]{1,0:T(4,128)S(1)}, u32[]{:S(2)}) copy-start(s32[4,144]{1,0:T(4,128)S(1)} %get-tuple-element.158) | copy-start | bytes 6916
  58.5 317.7 %copy-start.57 = (s32[4,144]{1,0:T(4,128)}, s32[4,144]{1,0:T(4,128)S(1)}, u32[]{:S(2)}) copy-start(s32[4,144]{1,0:T(4,128)S(1)} %get-tuple-element.156) | copy-start | bytes 6916
  350.4 16.1 %copy-start.61 = (s32[4,144]{1,0:T(4,128)S(1)}, s32[4,144]{1,0:T(4,128)}, u32[]{:S(2)}) copy-start(s32[4,144]{1,0:T(4,128)} %get-tuple-element.159) | copy-start | bytes 6916
  350.4 37.0 %collective-permute-start.1 = (bf16[2,4,144,12,64]{2,4,1,3,0:T(8,128)(2,1)}, bf16[2,4,144,12,64]{2,4,1,3,0:T(8,128)(2,1)}, u32[]{:S(2)}, u32[]{:S(2)}) collective-permute-start(bf16[2,4,144,12,64]{2,4,1,3,0:T(8,128)(2,1)} %collective-permute-done), channel_id=1, source_target_pairs={{0,1},{1,2},{2,3},{3,0},{4,5},{5,6},{6,7},{7,4},{8,9},{9,10},{10,1... | collective-permute-start | bytes 5308424 | tf_op jit(solution)/shard_map/ppermute | solution.py:22
  366.5 9.6 slice-start
  366.5 9.6 slice-start.1
  366.5 9.6 slice-start.2
  366.5 9.6 copy-start.44
  385.2 59.7 %copy-start.43 = (f32[12,4,144]{2,1,0:T(4,128)}, f32[12,4,144]{2,1,0:T(4,128)S(1)}, u32[]{:S(2)}) copy-start(f32[12,4,144]{2,1,0:T(4,128)S(1)} %get-tuple-element.179) | copy-start | bytes 82948
  387.4 37.1 %collective-permute-start.2 = (bf16[2,4,144,12,64]{2,4,1,3,0:T(8,128)(2,1)}, bf16[2,4,144,12,64]{2,4,1,3,0:T(8,128)(2,1)S(1)}, u32[]{:S(2)}, u32[]{:S(2)}) collective-permute-start(bf16[2,4,144,12,64]{2,4,1,3,0:T(8,128)(2,1)} %collective-permute-done.1), channel_id=1, source_target_pairs={{0,1},{1,2},{2,3},{3,0},{4,5},{5,6},{6,7},{7,4},{8,9},{9,10},{10,1... | collective-permute-start | bytes 5308424 | tf_op jit(solution)/shard_map/ppermute | solution.py:22
  391.7 12.4 slice-start.11
  391.7 12.4 slice-start.12
  404.1 20.4 %copy-start.45 = (pred[4,144,144]{1,2,0:T(8,128)(4,1)S(1)}, pred[4,144,144]{1,2,0:T(8,128)(4,1)}, u32[]{:S(2)}) copy-start(pred[4,144,144]{1,2,0:T(8,128)(4,1)} %get-tuple-element.170) | copy-start | bytes 248836
  407.6 32.4 %copy-start.6 = (f32[12,4,144,144]{2,3,1,0:T(8,128)}, f32[12,4,144,144]{2,3,1,0:T(8,128)S(1)}, u32[]{:S(2)}) copy-start(f32[12,4,144,144]{2,3,1,0:T(8,128)S(1)} %get-tuple-element.176) | copy-start | bytes 11943940
  430.7 9.4 copy-start.5
  430.7 9.3 copy-start.50
  430.7 9.4 copy-start.48
  430.8 9.4 copy-start.49
  500.3 14.2 %slice-start.13 = ((s8[4718592]{0:T(1024)(128)(4,1)}), s8[524288]{0:T(1024)(128)(4,1)S(1)}, s32[]{:S(2)}) async-start(s8[4718592]{0:T(1024)(128)(4,1)} %bitcast.328), calls=%async_computation.30 | async-start | bytes 1048576
  507.0 7.6 copy-start.35
  507.0 7.6 copy-start.36
  507.0 7.6 copy-start.38
  507.0 7.6 copy-start.65
  507.0 7.6 copy-start.76
  507.0 7.6 copy-start.86
  507.0 7.6 slice-start.14
  525.2 303.6 %reduce-scatter.23.cloned.1.call-start = ((), (), s32[]{:S(2)}) async-start(), calls=%async_computation.13 | async-start | bytes 10616832 | tf_op jit(solution)/shard_map/reduce_scatter | solution.py:261
  535.1 402.3 %reduce-scatter.19.cloned.1.call-start = ((), (), s32[]{:S(2)}) async-start(), calls=%async_computation.11 | async-start | bytes 10616832 | tf_op jit(solution)/shard_map/reduce_scatter | solution.py:260
  545.4 512.8 %reduce-scatter.15.cloned.1.call-start = ((), (), s32[]{:S(2)}) async-start(), calls=%async_computation.8 | async-start | bytes 7962624 | tf_op jit(solution)/shard_map/reduce_scatter | solution.py:258
  571.5 15.2 %copy-start.4 = (bf16[4,144,12,64]{1,0,3,2:T(4,128)(2,1)S(1)}, bf16[4,144,12,64]{1,0,3,2:T(4,128)(2,1)}, u32[]{:S(2)}) copy-start(bf16[4,144,12,64]{1,0,3,2:T(4,128)(2,1)} %reshape.326) | copy-start | bytes 2654212
  592.4 133.7 %copy-start.7 = (bf16[12,4,144,144]{2,3,1,0:T(8,128)(2,1)}, bf16[12,4,144,144]{2,3,1,0:T(8,128)(2,1)S(1)}, u32[]{:S(2)}) copy-start(bf16[12,4,144,144]{2,3,1,0:T(8,128)(2,1)S(1)} %multiply_convert_fusion.3) | copy-start | bytes 5971972
  596.0 37.2 %collective-permute-start.3 = (bf16[2,4,144,12,64]{2,4,3,1,0:T(8,128)(2,1)}, bf16[2,4,144,12,64]{2,4,3,1,0:T(8,128)(2,1)}, u32[]{:S(2)}, u32[]{:S(2)}) collective-permute-start(bf16[2,4,144,12,64]{2,4,3,1,0:T(8,128)(2,1)} %pad_maximum_fusion.1), channel_id=1, source_target_pairs={{0,1},{1,2},{2,3},{3,0},{4,5},{5,6},{6,7},{7,4},{8,9},{9,10},{10,1... | collective-permute-start | bytes 5308424 | tf_op jit(solution)/shard_map/ppermute | solution.py:22
  602.9 126.3 %copy-start.9 = (bf16[12,4,144,144]{2,3,1,0:T(8,128)(2,1)}, bf16[12,4,144,144]{2,3,1,0:T(8,128)(2,1)S(1)}, u32[]{:S(2)}) copy-start(bf16[12,4,144,144]{2,3,1,0:T(8,128)(2,1)S(1)} %multiply_convert_fusion.2) | copy-start | bytes 5971972
  603.0 40.0 %slice-start.5 = ((s8[7077888]{0:T(1024)(128)(4,1)}), s8[4194304]{0:T(1024)(128)(4,1)S(1)}, s32[]{:S(2)}) async-start(s8[7077888]{0:T(1024)(128)(4,1)} %bitcast.308), calls=%async_computation.22 | async-start | bytes 8388608
  606.1 34.0 %copy-start.21 = (bf16[12,4,144,144]{2,3,1,0:T(8,128)(2,1)S(1)}, bf16[12,4,144,144]{2,3,1,0:T(8,128)(2,1)}, u32[]{:S(2)}) copy-start(bf16[12,4,144,144]{2,3,1,0:T(8,128)(2,1)} %get-tuple-element.152) | copy-start | bytes 5971972
  606.1 36.9 %slice-start.6 = ((s8[7077888]{0:T(1024)(128)(4,1)}), s8[2883584]{0:T(1024)(128)(4,1)S(1)}, s32[]{:S(2)}) async-start(s8[7077888]{0:T(1024)(128)(4,1)} %bitcast.308), calls=%async_computation.23 | async-start | bytes 5767168
  640.0 37.0 %collective-permute-start.4 = (bf16[2,4,144,12,64]{2,4,3,1,0:T(8,128)(2,1)}, bf16[2,4,144,12,64]{2,4,3,1,0:T(8,128)(2,1)}, u32[]{:S(2)}, u32[]{:S(2)}) collective-permute-start(bf16[2,4,144,12,64]{2,4,3,1,0:T(8,128)(2,1)} %fusion.15), channel_id=1, source_target_pairs={{0,1},{1,2},{2,3},{3,0},{4,5},{5,6},{6,7},{7,4},{8,9},{9,10},{10,1... | collective-permute-start | bytes 5308424 | tf_op jit(solution)/shard_map/ppermute | solution.py:22
  646.4 40.9 %slice-start.3 = ((s8[7077888]{0:T(1024)(128)(4,1)}), s8[4194304]{0:T(1024)(128)(4,1)S(1)}, s32[]{:S(2)}) async-start(s8[7077888]{0:T(1024)(128)(4,1)} %bitcast.306), calls=%async_computation.20 | async-start | bytes 8388608
  649.8 37.5 %slice-start.4 = ((s8[7077888]{0:T(1024)(128)(4,1)}), s8[2883584]{0:T(1024)(128)(4,1)S(1)}, s32[]{:S(2)}) async-start(s8[7077888]{0:T(1024)(128)(4,1)} %bitcast.306), calls=%async_computation.21 | async-start | bytes 5767168
  684.0 37.2 %collective-permute-start.5 = (bf16[2,4,144,12,64]{2,4,3,1,0:T(8,128)(2,1)}, bf16[2,4,144,12,64]{2,4,3,1,0:T(8,128)(2,1)}, u32[]{:S(2)}, u32[]{:S(2)}) collective-permute-start(bf16[2,4,144,12,64]{2,4,3,1,0:T(8,128)(2,1)} %fusion.16), channel_id=1, source_target_pairs={{0,1},{1,2},{2,3},{3,0},{4,5},{5,6},{6,7},{7,4},{8,9},{9,10},{10,1... | collective-permute-start | bytes 5308424 | tf_op jit(solution)/shard_map/ppermute | solution.py:22
  690.6 40.1 %copy-start.8 = (bf16[12,4,144,144]{2,3,1,0:T(8,128)(2,1)}, bf16[12,4,144,144]{2,3,1,0:T(8,128)(2,1)S(1)}, u32[]{:S(2)}) copy-start(bf16[12,4,144,144]{2,3,1,0:T(8,128)(2,1)S(1)} %multiply_convert_fusion) | copy-start | bytes 5971972
  690.6 30.6 %copy-start.25 = (f32[1,4,144,12,64]{2,4,3,1,0:T(8,128)S(1)}, f32[1,4,144,12,64]{2,4,3,1,0:T(8,128)}, u32[]{:S(2)}) copy-start(f32[1,4,144,12,64]{2,4,3,1,0:T(8,128)} %fusion.96) | copy-start | bytes 5308420
  691.9 34.2 %copy-start.16 = (bf16[4,144,12,64]{1,0,3,2:T(4,128)(2,1)S(1)}, bf16[4,144,12,64]{1,0,3,2:T(4,128)(2,1)}, u32[]{:S(2)}) copy-start(bf16[4,144,12,64]{1,0,3,2:T(4,128)(2,1)} %squeeze_stack_reshape.4) | copy-start | bytes 2654212
  726.1 37.0 %collective-permute-start.6 = (bf16[2,4,144,12,64]{2,4,3,1,0:T(8,128)(2,1)}, bf16[2,4,144,12,64]{2,4,3,1,0:T(8,128)(2,1)}, u32[]{:S(2)}, u32[]{:S(2)}) collective-permute-start(bf16[2,4,144,12,64]{2,4,3,1,0:T(8,128)(2,1)} %fusion.17), channel_id=1, source_target_pairs={{0,1},{1,2},{2,3},{3,0},{4,5},{5,6},{6,7},{7,4},{8,9},{9,10},{10,1... | collective-permute-start | bytes 5308424 | tf_op jit(solution)/shard_map/ppermute | solution.py:22
  792.0 366.2 %reduce-scatter.27.cloned.1.call-start = ((), (), s32[]{:S(2)}) async-start(), calls=%async_computation.15 | async-start | bytes 245760
  794.6 11.4 copy-start.12
  794.6 11.4 copy-start.60
  806.0 11.6 copy-start.58
  817.6 395.4 %reduce-scatter.29.cloned.1.call-start = ((), (), s32[]{:S(2)}) async-start(), calls=%async_computation.16 | async-start | bytes 737280
  833.1 383.4 %reduce-scatter.21.cloned.1.call-start = ((), (), s32[]{:S(2)}) async-start(), calls=%async_computation.12 | async-start | bytes 737280 | tf_op jit(solution)/shard_map/reduce_scatter | solution.py:270
  939.7 278.4 %reduce-scatter.25.cloned.1.call-start = ((), (), s32[]{:S(2)}) async-start(), calls=%async_computation.14 | async-start | bytes 737280
  1062.3 98.8 %copy-start.70 = (f32[576]{0:T(1024)S(1)}, f32[576]{0:T(1024)}, u32[]{:S(2)}) copy-start(f32[576]{0:T(1024)} %copy-done.69) | copy-start | bytes 6916
  1062.3 98.8 %copy-start.72 = (f32[768]{0:T(1024)S(1)}, f32[768]{0:T(1024)}, u32[]{:S(2)}) copy-start(f32[768]{0:T(1024)} %copy-done.71) | copy-start | bytes 9220
  1062.3 98.8 %copy-start.74 = (f32[576]{0:T(1024)S(1)}, f32[576]{0:T(1024)}, u32[]{:S(2)}) copy-start(f32[576]{0:T(1024)} %copy-done.73) | copy-start | bytes 6916
  1062.3 219.5 %all-reduce.3.cloned.1.call-start = ((), (), s32[]{:S(2)}) async-start(), calls=%async_computation.9 | async-start | bytes 294912 | tf_op jit(solution)/shard_map/psum | solution.py:277
  (56 other events, 233.3 us)
Sparse Core Ops, SparseCore 0:
  525.3 69.5 reduce-scatter.16
  598.5 161.5 reduce-scatter.22
  763.7 162.3 reduce-scatter.18
  929.7 128.4 reduce-scatter.14
  1061.2 19.7 reduce-scatter.26
  1083.5 22.0 reduce-scatter.28
  1108.3 22.0 reduce-scatter.20
  1133.0 22.0 reduce-scatter.24
Sparse Core Ops, SparseCore 1:
  1158.2 123.5 all-reduce.2
where the time goes:
time: 1300 us; the launch traced here: 1290 us
  matrix products  495 us (38%)
  local copies, waits for them, and re-layouts  385 us (30%)
  waiting for transfers between devices  229 us (18%)
  other arithmetic  120 us (9%)
  blocking collectives  41.9 us (3%)
  between operations  17.3 us (1%)
    dot_general x46, matrix products, product(): return jnp.einsum(form, left, right, preferred_element_type=jnp.float32)  328 us
    ppermute x7, waiting for transfers between devices, shifted(): return lax.ppermute(value, axis, pairs)  123 us
    dot_general x1, matrix products, on_device(): jnp.einsum('nra,nrbh->abh', row_pick.astype(jnp.float32), slab_change, pr...  92.6 us
    reshape x2, local copies, waits for them, and re-layouts, on_device(): window_grid = window_sum.reshape(rows * width_slots, GRID, GRID, HEADS)  75.4 us
    dot_general x1, matrix products, on_device(): jnp.einsum('nrch,ncb->nrbh', window_grid, column_pick.astype(jnp.float32)...  73.6 us
    convert_element_type x1, local copies, waits for them, and re-layouts, on_device(): product(row_pick.astype(jnp.bfloat16), table_grid, 'nra,abh->nrbh')  71.9 us
    psum x1, waiting for transfers between devices, on_device(): lax.psum((first_gain_gradient, first_shift_gradient, query_bias_gradient,...  60.4 us
    reshape x2, local copies, waits for them, and re-layouts, on_device(): window = window.reshape(rows, width_slots, GRID * GRID, HEADS)  50.7 us
  transfers between devices with their start and end apart: 16, of which 8 were waited for; matrix products, arithmetic and copies ran while one was open for 66% of the time, Pallas kernels for 0%

commit v1 on v0

v1 whole, which is shorter than its diff:
```python
import functools
import math

import jax
import jax.numpy as jnp
from jax import lax
from jax.experimental import pallas as pl
from jax.experimental.pallas import tpu as pltpu
from jax.sharding import PartitionSpec as P

HEADS = 12
HEAD = 64
GRID = 24
SPAN = 2 * GRID - 1
SLOTS = 576
PADDED = 640
MODEL = 768
PAIRS = HEADS // 2
WIDE = 1152
STRIP = 128
BASE = 489
COMPACT = 32
IMGS = 4
EPS = 1e-06
NEGATIVE = -1e30
CHUNK = 32
F32 = jnp.float32
BF16 = jnp.bfloat16
VMEM_LIMIT = 62 * 2**20


def dot(left, right):
    return lax.dot_general(left, right, (((1,), (0,)), ((), ())), preferred_element_type=F32)


def dot_nt(left, right):
    return lax.dot_general(left, right, (((1,), (1,)), ((), ())), preferred_element_type=F32)


def dot_tn(left, right):
    return lax.dot_general(left, right, (((0,), (0,)), ((), ())), preferred_element_type=F32)


def chunks(body):
    def step(index, carry):
        body(pl.ds(pl.multiple_of(index * CHUNK, CHUNK), CHUNK))
        return carry

    lax.fori_loop(0, SLOTS // CHUNK, step, 0)


def fold(value):
    return jnp.sum(value.reshape(value.shape[0] // 8, 8, value.shape[1]), 0)


def normal_of(values):
    center = values - jnp.mean(values, -1, keepdims=True)
    spread = lax.rsqrt(jnp.mean(center * center, -1, keepdims=True) + EPS)
    return center * spread, spread


def normal_back(change, normal, spread, gain):
    scaled = change * gain
    inner = (
        scaled
        - jnp.mean(scaled, -1, keepdims=True)
        - normal * jnp.mean(scaled * normal, -1, keepdims=True)
    )
    return inner * spread


def row_scalars(heights, widths, order, row):
    sizes, breadths, large = [], [], []
    for place in range(IMGS):
        picked = order[row, place]
        size, breadth = jnp.int32(0), jnp.int32(0)
        for image in range(IMGS):
            hit = picked == image
            size = size + jnp.where(hit, heights[row, image] * widths[row, image], 0)
            breadth = breadth + jnp.where(hit, widths[row, image], 0)
        sizes.append(size)
        breadths.append(breadth)
        large.append(jnp.where(picked == 0, 1, 0))
    begins = [jnp.int32(0)]
    for place in range(IMGS - 1):
        begins.append(begins[-1] + sizes[place])
    large_begin = sum(begins[p] * large[p] for p in range(IMGS))
    return dict(
        sizes=sizes,
        breadths=breadths,
        large=large,
        begins=begins,
        large_begin=large_begin,
        large_size=heights[row, 0] * widths[row, 0],
        large_width=widths[row, 0],
    )


def place_info(info, slot):
    segment = jnp.full(slot.shape, IMGS, jnp.int32)
    across = jnp.zeros(slot.shape, jnp.int32)
    down = jnp.zeros(slot.shape, jnp.int32)
    large = jnp.zeros(slot.shape, jnp.int32)
    for place in range(IMGS):
        offset = slot - info["begins"][place]
        inside = (offset >= 0) & (offset < info["sizes"][place])
        breadth = jnp.full(slot.shape, info["breadths"][place], jnp.int32)
        line = ((offset.astype(F32) + 0.5) / breadth.astype(F32)).astype(jnp.int32)
        segment = jnp.where(inside, place, segment)
        down = jnp.where(inside, line, down)
        across = jnp.where(inside, offset - line * breadth, across)
        large = jnp.where(inside, info["large"][place], large)
    return segment, down, across, large


def compact_index(info):
    found = []
    for axis in (0, 1):
        number = lax.broadcasted_iota(jnp.int32, (COMPACT, 128), axis)
        slot = number + jnp.where(number >= info["large_begin"], info["large_size"], 0)
        segment, down, across, large = place_info(info, slot)
        small = (segment < IMGS) & (large == 0) & (number < COMPACT)
        found.append((jnp.where(small, segment, -1 - axis), down, across))
    same = found[0][0] == found[1][0]
    row_step = found[0][1] - found[1][1] + 2
    column_step = found[0][2] - found[1][2] + 2
    return jnp.where(same, row_step * 5 + column_step, -1)


def shift_of(info, line):
    shift = BASE - (line - (GRID - 1)) * info["large_width"]
    return jnp.where(shift < 0, shift + WIDE, shift)


def prepare(info, reversed_table, near_table, picks, query_codes, key_code, bands, near):
    def rows(index, carry):
        start = pl.multiple_of(index * 64, 64)
        slot = lax.broadcasted_iota(jnp.int32, (64, 128), 0) + start
        lane = lax.broadcasted_iota(jnp.int32, (64, 128), 1)
        segment, _, across, large = place_info(info, slot)
        rank = slot - jnp.where(slot >= info["large_begin"], info["large_size"], 0)
        small = (segment < IMGS) & (large == 0)
        target = jnp.where(small, rank, -1)
        pick = (lane == target) | (lane == segment + COMPACT)
        picks[pl.ds(start, 64), :] = jnp.where(pick, 1.0, 0.0).astype(BF16)
        code = across.astype(F32)
        query_codes[0, pl.ds(start, 64), :] = jnp.where(large == 1, code, -1e9)
        query_codes[1, pl.ds(start, 64), :] = jnp.where(large == 1, code, 1e9)
        return carry

    lax.fori_loop(0, SLOTS // 64, rows, 0)
    slot = lax.broadcasted_iota(jnp.int32, (8, PADDED), 1)
    key_code[...] = place_info(info, slot)[2].astype(F32)

    lanes = lax.broadcasted_iota(jnp.int32, (16, WIDE), 1)
    width = info["large_width"]

    def line_step(line, carry):
        low, high = carry
        shift = shift_of(info, line)
        wide = jnp.concatenate([reversed_table[line], jnp.zeros((16, WIDE - 128), F32)], 1)
        rolled = pltpu.roll(wide, shift, 1)
        entry = lanes - shift
        entry = jnp.where(entry < 0, entry + WIDE, entry)
        low = jnp.where((entry >= GRID - width) & (entry <= GRID - 1), rolled, low)
        high = jnp.where((entry >= GRID) & (entry <= GRID - 2 + width), rolled, high)
        return low, high

    zero = jnp.zeros((16, WIDE), F32)
    low, high = lax.fori_loop(0, SPAN, line_step, (zero, zero))
    for head in range(HEADS):
        bands[head, 0] = jnp.broadcast_to(low[head : head + 1], (8, WIDE))
        bands[head, 1] = jnp.broadcast_to(high[head : head + 1], (8, WIDE))

    index = compact_index(info)
    across = lax.broadcasted_iota(jnp.int32, (128 - COMPACT, 128), 1) - COMPACT
    down = lax.broadcasted_iota(jnp.int32, (128 - COMPACT, 128), 0)
    inside = (across >= 0) & (across <= IMGS) & (down <= IMGS)
    for head in range(HEADS):
        value = jnp.zeros((COMPACT, 128), F32)
        for entry in range(25):
            value = jnp.where(index == entry, near_table[entry, head], value)
        near[head, 0:COMPACT, :] = value.astype(BF16)
        own = jnp.where(down == IMGS, near_table[12, head], 0.0)
        lower = jnp.where(inside, jnp.where(across == down, own, NEGATIVE), 0.0)
        near[head, COMPACT:128, :] = lower.astype(BF16)


def project_in(tokens, gain, shift, weight, query_bias, value_bias, first, query, keys, values):
    def norm(rows):
        normal, _ = normal_of(tokens[rows, :].astype(F32))
        first[rows, :] = (normal * gain[...] + shift[...]).astype(BF16)

    chunks(norm)
    step = 256
    for part, out in enumerate((query, keys, values)):
        for block in range(MODEL // step):
            lanes = slice(block * step, (block + 1) * step)
            columns = slice(part * MODEL + block * step, part * MODEL + (block + 1) * step)
            mixed = dot(first[...], weight[:, columns])
            if part == 0:
                mixed = (mixed + query_bias[:, lanes]) * HEAD**-0.5
            if part == 2:
                mixed = mixed + value_bias[:, lanes]
            out[:, lanes] = mixed.astype(BF16)


def half_mask(half):
    lane = lax.broadcasted_iota(jnp.int32, (SLOTS, 128), 1)
    return (lane < HEAD) if half == 0 else (lane >= HEAD)


def keep(mask, value):
    return jnp.where(mask, value, jnp.zeros_like(value))


def attend(query, keys, values, picks, query_codes, key_code, bands, near, chance, attended, inverse, score, low_strip, high_strip):
    def pair_step(pair, carry):
        lanes = pl.ds(pl.multiple_of(pair * 128, 128), 128)
        key_side = jnp.concatenate([keys[:, lanes], picks[...]], 1)
        result = jnp.zeros((SLOTS, 256), F32)
        for half in range(2):
            head = pair * 2 + half
            mask = half_mask(half)
            near_side = dot(picks[...], near[head]).astype(BF16)
            query_side = jnp.concatenate([keep(mask, query[:, lanes]), near_side], 1)
            score[...] = dot_nt(query_side, key_side)
            for which, strip in enumerate((low_strip, high_strip)):
                band = jnp.concatenate([bands[head, which]] * (STRIP // 8), 0)
                strip[...] = pltpu.roll(band, 0, 1, stride=1, stride_axis=0)
            for block in range(SLOTS // 64):
                rows = slice(block * 64, (block + 1) * 64)
                strip_rows = slice(block % 2 * 64, block % 2 * 64 + 64)
                start = 512 - block // 2 * 128
                strip_lanes = slice(start, start + SLOTS)
                code = key_code[0:1, 0:SLOTS]
                low_hit = query_codes[0, rows, 0:1] >= code
                high_hit = code > query_codes[1, rows, 0:1]
                bias = jnp.where(
                    low_hit,
                    low_strip[strip_rows, strip_lanes],
                    jnp.where(high_hit, high_strip[strip_rows, strip_lanes], 0.0),
                )
                part = score[rows, :] + bias
                top = jnp.max(part, -1, keepdims=True)
                chance[head, rows, 0:SLOTS] = jnp.exp(part - top).astype(BF16)
            chance[head, :, SLOTS:] = jnp.zeros((SLOTS, PADDED - SLOTS), BF16)
            value_side = jnp.concatenate(
                [keep(mask, values[:, lanes]), keep(mask, jnp.ones((SLOTS, 128), BF16))], 1
            )
            result = result + dot(chance[head, :, 0:SLOTS], value_side)
        scale = 1.0 / result[:, 128:]
        inverse[:, lanes] = scale
        attended[:, lanes] = result[:, :128] * scale
        return carry

    lax.fori_loop(0, PAIRS, pair_step, 0)


def project_out(tokens, attended, weight, bias, scale, gain, shift, branch, middle, second, attended_low):
    attended_low[...] = attended[...].astype(BF16)
    step = 256
    for block in range(MODEL // step):
        lanes = slice(block * step, (block + 1) * step)
        branch[:, lanes] = dot(attended_low[...], weight[:, lanes]) + bias[:, lanes]

    def norm(rows):
        value = tokens[rows, :].astype(F32) + scale[...] * branch[rows, :]
        middle[rows, :] = value
        normal, _ = normal_of(value)
        second[rows, :] = (normal * gain[...] + shift[...]).astype(BF16)

    chunks(norm)


def gelu_parts(value):
    square = value * value
    bell = jnp.exp(square * -0.5)
    base = 1.0 + (0.3275911 / math.sqrt(2.0)) * jnp.abs(value)
    guess = pl.reciprocal(base, approx=True)
    inner = guess * (2.0 - base * guess)
    poly = 1.061405429
    for coefficient in (-1.453152027, 1.421413741, -0.284496736, 0.254829592):
        poly = poly * inner + coefficient
    tail = 0.5 * poly * inner * bell
    share = jnp.where(value >= 0.0, 1.0 - tail, tail)
    return value * share, share + value * bell * (1.0 / math.sqrt(2.0 * math.pi))


def feed_tile(second, outcome_change, up, up_bias, down, active, slope, hidden, change):
    hidden[...] = dot(second[...], up[...]) + up_bias
    change[...] = dot_nt(outcome_change[...], down[...])

    def body(rows):
        value, gradient = gelu_parts(hidden[rows, :])
        active[rows, :] = value.astype(BF16)
        slope[rows, :] = (change[rows, :] * gradient).astype(BF16)

    chunks(body)


def feed_kernel(second, middle, upstream, up, up_bias, down, down_bias, feed_scale, output, second_change, up_unit, down_unit, up_sum, feed_sums, outcome_change, outcome, active, slope, hidden, change):
    tile = pl.program_id(0)

    @pl.when(tile == 0)
    def _():
        feed_sums[...] = jnp.zeros_like(feed_sums)

        def body(rows):
            value = (upstream[rows, :].astype(F32) * feed_scale[...]).astype(BF16)
            outcome_change[rows, :] = value
            feed_sums[1] += fold(value.astype(F32))

        chunks(body)

    feed_tile(second, outcome_change, up, up_bias[...], down, active, slope, hidden, change)
    up_unit[0] = dot_tn(second[...], slope[...]).astype(BF16)
    turned = dot_tn(outcome_change[...], active[...]).astype(BF16)
    for part in range(4):
        for half in range(2):
            down_unit[part, half] = turned[part * 192 : part * 192 + 192, half * 384 : half * 384 + 384]
    result = dot(active[...], down[...])
    back = dot_nt(slope[...], up[...])

    @pl.when(tile == 0)
    def _():
        outcome[...] = result
        second_change[...] = back

    @pl.when(tile > 0)
    def _():
        outcome[...] += result
        second_change[...] += back

    up_sum[...] = jnp.zeros_like(up_sum)

    def sums(rows):
        up_sum[0] += fold(slope[rows, :].astype(F32))

    chunks(sums)

    @pl.when(tile == pl.num_programs(0) - 1)
    def _():
        def body(rows):
            value = outcome[rows, :] + down_bias[...]
            output[rows, :] = (middle[rows, :] + feed_scale[...] * value).astype(BF16)
            feed_sums[0] += fold(upstream[rows, :].astype(F32) * value)

        chunks(body)


def attend_back(query, keys, values, picks, query_codes, key_code, chance, change_low, attended, inverse, joined, band_sums, near_sums, weight_change, score_change):
    def pair_step(pair, carry):
        lanes = pl.ds(pl.multiple_of(pair * 128, 128), 128)
        key_lanes = pl.ds(pl.multiple_of(pair * 128 + MODEL, 128), 128)
        value_lanes = pl.ds(pl.multiple_of(pair * 128 + 2 * MODEL, 128), 128)
        lane = lax.broadcasted_iota(jnp.int32, (SLOTS, 128), 1)
        own_change = change_low[:, lanes].astype(F32)
        scale = inverse[:, lanes]
        terms = own_change * attended[:, lanes]
        high = terms.astype(BF16)
        low = (terms - high.astype(F32)).astype(BF16)
        block_row = lax.broadcasted_iota(jnp.int32, (128, 128), 0) // HEAD
        block_lane = lax.broadcasted_iota(jnp.int32, (128, 128), 1) // HEAD
        block = jnp.where(block_row == block_lane, 1.0, 0.0).astype(BF16)
        delta = (dot(high, block) + dot(low, block)) * -scale
        delta_high = delta.astype(BF16)
        delta_low = (delta - delta_high.astype(F32)).astype(BF16)
        scaled = (own_change * scale).astype(BF16)
        value_side = jnp.concatenate([values[:, lanes], jnp.ones((SLOTS, 128), BF16)], 1)
        query_total = jnp.zeros((SLOTS, 128), F32)
        key_total = jnp.zeros((SLOTS, 128), F32)
        value_total = jnp.zeros((SLOTS, 128), F32)
        for half in range(2):
            head = pair * 2 + half
            mask = half_mask(half)
            extra = jnp.where(
                lane == half * HEAD,
                delta_high,
                jnp.where(lane == half * HEAD + 1, delta_low, jnp.zeros_like(delta_low)),
            )
            own_scaled = keep(mask, scaled)
            weight_change[:, 0:SLOTS] = dot_nt(jnp.concatenate([own_scaled, extra], 1), value_side)
            kinds = [jnp.zeros((16, WIDE), F32), jnp.zeros((16, WIDE), F32)]
            for group in range(STRIP // 16 - 1, -1, -1):
                tiles = [[jnp.zeros((16, 128), F32)] * (WIDE // 128) for _ in range(2)]
                for major in range(-(-SLOTS // STRIP)):
                    start = major * STRIP + group * 16
                    if start >= SLOTS:
                        continue
                    rows = slice(start, start + 16)
                    low_code = query_codes[0, rows, :]
                    high_code = query_codes[1, rows, :]
                    for column in range(-(-SLOTS // 128)):
                        span = slice(column * 128, column * 128 + 128)
                        value = chance[head, rows, span].astype(F32) * weight_change[rows, span]
                        code = jnp.broadcast_to(key_code[0:1, span], (16, 128))
                        if column * 128 + 128 > SLOTS:
                            inside = lax.broadcasted_iota(jnp.int32, (16, 128), 1) < SLOTS - column * 128
                            value = jnp.where(inside, value, 0.0)
                        score_change[rows, span] = value.astype(BF16)
                        place = 4 - major + column
                        tiles[0][place] = tiles[0][place] + jnp.where(low_code >= code, value, 0.0)
                        tiles[1][place] = tiles[1][place] + jnp.where(code > high_code, value, 0.0)
                for which in range(2):
                    fresh = jnp.concatenate(tiles[which], 1)
                    if group == STRIP // 16 - 1:
                        kinds[which] = fresh
                    else:
                        kinds[which] = pltpu.roll(kinds[which], WIDE - 16, 1) + fresh
            for which in range(2):
                band_sums[head, which] = kinds[which][0:8] + pltpu.roll(kinds[which][8:16], WIDE - 8, 1)
            own_score = score_change[:, 0:SLOTS]
            key_side = jnp.concatenate([keep(mask, keys[:, lanes]), picks[...]], 1)
            both = dot(own_score, key_side)
            query_total = query_total + both[:, :128]
            near_sums[head] = dot_tn(picks[...], both[:, 128:].astype(BF16))
            key_total = key_total + dot_tn(own_score, keep(mask, query[:, lanes]))
            value_total = value_total + dot_tn(chance[head, :, 0:SLOTS], own_scaled)
        joined[:, lanes] = (query_total.astype(BF16).astype(F32) * HEAD**-0.5).astype(BF16)
        joined[:, key_lanes] = key_total.astype(BF16)
        joined[:, value_lanes] = value_total.astype(BF16)
        return carry

    lax.fori_loop(0, PAIRS, pair_step, 0)


def table_back(info, band_sums, near_sums, table_sum):
    kinds = []
    for which in range(2):
        total = jnp.zeros((16, WIDE), F32)
        for step in range(8):
            rows = jnp.concatenate(
                [band_sums[head, which, step : step + 1, :] for head in range(HEADS)]
                + [jnp.zeros((16 - HEADS, WIDE), F32)],
                0,
            )
            total = total + (rows if step == 0 else pltpu.roll(rows, WIDE - step, 1))
        kinds.append(total)
    low, high = kinds
    width = info["large_width"]
    entry = lax.broadcasted_iota(jnp.int32, (16, 128), 1)
    low_hit = (entry >= GRID - width) & (entry <= GRID - 1)
    high_hit = (entry >= GRID) & (entry <= GRID - 2 + width)

    def line_step(line, carry):
        back = WIDE - shift_of(info, line)
        low_part = pltpu.roll(low, back, 1)[:, :128]
        high_part = pltpu.roll(high, back, 1)[:, :128]
        table_sum[line] = jnp.where(low_hit, low_part, jnp.where(high_hit, high_part, 0.0))
        return carry

    lax.fori_loop(0, SPAN, line_step, 0)
    index = compact_index(info)
    head_row = lax.broadcasted_iota(jnp.int32, (16, 128), 0)
    for row_step in range(5):
        addition = jnp.zeros((16, 128), F32)
        for column_step in range(5):
            hit = index == row_step * 5 + column_step
            column = jnp.zeros((16, 128), F32)
            for head in range(HEADS):
                part = jnp.sum(jnp.where(hit, near_sums[head, 0:COMPACT, :], 0.0), 0, keepdims=True)
                column = jnp.where(head_row == head, part, column)
            total = jnp.sum(column, 1, keepdims=True)
            addition = addition + jnp.where(entry == GRID + 1 - column_step, total, 0.0)
        if row_step == 2:
            corner = jnp.zeros((16, 128), F32)
            for head in range(HEADS):
                at = COMPACT + IMGS
                own = near_sums[head, at : at + 1, :]
                corner = jnp.where(head_row == head, own, corner)
            own = jnp.sum(jnp.where(entry == COMPACT + IMGS, corner, 0.0), 1, keepdims=True)
            addition = addition + jnp.where(entry == GRID - 1, own, 0.0)
        table_sum[GRID - 3 + row_step] += addition


def forward_kernel(heights, widths, order, near_table, reversed_table, tokens, first_gain, first_shift, input_weight, query_bias, value_bias, output_weight, output_bias, attention_scale, second_gain, second_shift, first, query, keys, values, chance, attended, inverse, branch, middle, second, attended_low, picks, query_codes, key_code, bands, near, score, low_strip, high_strip):
    info = row_scalars(heights, widths, order, lax.axis_index("seq"))
    prepare(info, reversed_table, near_table, picks, query_codes, key_code, bands, near)
    project_in(tokens, first_gain, first_shift, input_weight, query_bias, value_bias, first, query, keys, values)
    attend(query, keys, values, picks, query_codes, key_code, bands, near, chance, attended, inverse, score, low_strip, high_strip)
    project_out(tokens, attended, output_weight, output_bias, attention_scale, second_gain, second_shift, branch, middle, second, attended_low)


def backward_kernel(heights, widths, order, tokens, upstream, middle, branch, second_change, attended, attended_low, inverse, first, query, keys, values, chance, picks, query_codes, key_code, input_weight, output_weight, attention_scale, second_gain, first_gain, gradient, input_unit, output_unit, table_sum, sums, middle_change, branch_change, change_low, joined, band_sums, near_sums, weight_change, score_change, first_change):
    info = row_scalars(heights, widths, order, lax.axis_index("seq"))
    sums[...] = jnp.zeros_like(sums)

    def norm(rows):
        normal, spread = normal_of(middle[rows, :])
        change = second_change[rows, :]
        sums[6] += fold(change * normal)
        sums[7] += fold(change)
        value = upstream[rows, :].astype(F32) + normal_back(change, normal, spread, second_gain[...])
        middle_change[rows, :] = value
        sums[5] += fold(value * branch[rows, :])
        low = (value * attention_scale[...]).astype(BF16)
        branch_change[rows, :] = low
        sums[4] += fold(low.astype(F32))

    chunks(norm)
    for part in range(4):
        output_unit[part] = dot_tn(attended_low[...], branch_change[:, part * 192 : part * 192 + 192]).astype(BF16)
    change_low[...] = dot_nt(branch_change[...], output_weight[...]).astype(BF16)
    attend_back(query, keys, values, picks, query_codes, key_code, chance, change_low, attended, inverse, joined, band_sums, near_sums, weight_change, score_change)
    table_back(info, band_sums, near_sums, table_sum)
    for part in range(4):
        input_unit[part] = dot_tn(first[...], joined[:, part * 576 : part * 576 + 576]).astype(BF16)
    first_change[...] = dot_nt(joined[...], input_weight[...])

    def norm_first(rows):
        normal, spread = normal_of(tokens[rows, :].astype(F32))
        change = first_change[rows, :]
        sums[0] += fold(change * normal)
        sums[1] += fold(change)
        sums[2] += fold(joined[rows, 0:MODEL].astype(F32))
        sums[3] += fold(joined[rows, 2 * MODEL : 3 * MODEL].astype(F32))
        value = middle_change[rows, :] + normal_back(change, normal, spread, first_gain[...])
        gradient[rows, :] = value.astype(BF16)

    chunks(norm_first)


def remote(source, target, send, receive, device):
    return pltpu.make_async_remote_copy(
        src_ref=source,
        dst_ref=target,
        send_sem=send,
        recv_sem=receive,
        device_id=device,
        device_id_type=pl.DeviceIdType.MESH,
    )


def greet(devices):
    barrier = pltpu.get_barrier_semaphore()
    for device in devices:
        pl.semaphore_signal(barrier, inc=1, device_id=device, device_id_type=pl.DeviceIdType.MESH)
    pl.semaphore_wait(barrier, len(devices))


def spread_kernel(parts, tokens, upstream, full_tokens, full_upstream, send, receive, local):
    row, me = lax.axis_index("rows"), lax.axis_index("seq")
    peers = [lax.rem(me + step, parts) for step in range(1, parts)]
    greet([(row, peer) for peer in peers])
    slots = tokens.shape[1]
    mine = pl.ds(pl.multiple_of(me * slots, slots), slots)
    copies = []
    for which, (source, target) in enumerate(((tokens, full_tokens), (upstream, full_upstream))):
        for step, peer in enumerate(peers):
            copies.append(remote(source.at[peer], target.at[mine], send.at[which, step], receive.at[which, step], (row, peer)))
        copies.append(pltpu.make_async_copy(source.at[me], target.at[mine], local.at[which]))
    for copy in copies:
        copy.start()
    for copy in copies:
        copy.wait()


def gather_kernel(parts, output, gradient, own_output, own_gradient, send, receive, local):
    row, me = lax.axis_index("rows"), lax.axis_index("seq")
    peers = [lax.rem(me + step, parts) for step in range(1, parts)]
    greet([(row, peer) for peer in peers])
    slots = own_output.shape[1]
    copies = []
    for which, (source, target) in enumerate(((output, own_output), (gradient, own_gradient))):
        for step, peer in enumerate(peers):
            theirs = pl.ds(pl.multiple_of(peer * slots, slots), slots)
            copies.append(remote(source.at[theirs], target.at[me], send.at[which, step], receive.at[which, step], (row, peer)))
        mine = pl.ds(pl.multiple_of(me * slots, slots), slots)
        copies.append(pltpu.make_async_copy(source.at[mine], target.at[me], local.at[which]))
    for copy in copies:
        copy.start()
    for copy in copies:
        copy.wait()


UNITS = ((96, 576), (96, 192), (96, 768), (192, 384))
SMALL_ROWS = 512


def reduce_kernel(*refs):
    count = len(UNITS)
    units, small = refs[:count], refs[count]
    outs, small_out = refs[count + 1 : 2 * count + 1], refs[2 * count + 1]
    scratch = refs[2 * count + 2 :]
    core_in, x_in, y_in, late, line_in = (scratch[i * count : (i + 1) * count] for i in range(5))
    small_core, small_plane, small_line, small_part, send, receive, small_send, small_receive = scratch[5 * count :]
    rows, seq = lax.axis_index("rows"), lax.axis_index("seq")
    z, x = rows // 2, rows % 2
    y, core = seq // 2, seq % 2
    core_peer = (rows, y * 2 + 1 - core)
    x_peer = (z * 2 + 1 - x, seq)
    y_peer = (rows, (1 - y) * 2 + core)
    diagonal = (z * 2 + 1 - x, (1 - y) * 2 + core)
    z_peers = [(lax.rem(z + step, 4) * 2 + x, seq) for step in range(1, 4)]
    greet([core_peer, x_peer, y_peer, diagonal] + z_peers)

    small_core_copy = remote(small.at[1 - core], small_core, small_send.at[0], small_receive.at[0], core_peer)
    small_core_copy.start()
    core_copies = []
    for unit in range(count):
        for part in range(2):
            copy = remote(
                units[unit].at[part * 2 + 1 - core], core_in[unit].at[part],
                send.at[unit, part], receive.at[unit, part], core_peer,
            )
            copy.start()
            core_copies.append(copy)

    small_core_copy.wait()
    small_core[...] += small[core]
    plane = x * 2 + y
    plane_peers = ((x_peer, lax.rem(plane + 2, 4)), (y_peer, plane + 1 - 2 * y), (diagonal, 3 - plane))
    small_plane_copies = []
    for step, (peer, index) in enumerate(plane_peers):
        copy = remote(small_core.at[index], small_plane.at[step], small_send.at[1 + step], small_receive.at[1 + step], peer)
        copy.start()
        small_plane_copies.append(copy)

    first_copies = []
    for unit in range(count):
        half = UNITS[unit][0] // 2
        for part in range(2):
            core_copies[unit * 2 + part].wait()
        held = core_in[unit]

        def add(index, carry, held=held, unit=unit):
            line = index // 2
            for part in range(2):
                held[part, line, index % 2] = (
                    held[part, line, index % 2].astype(F32)
                    + units[unit][part * 2 + core, line, index % 2].astype(F32)
                ).astype(BF16)
            return carry

        lax.fori_loop(0, 8, add, 0)
        copy_x = remote(
            held.at[:, :, 1 - x, 0:half], x_in[unit], send.at[unit, 2], receive.at[unit, 2], x_peer
        )
        copy_y = remote(
            held.at[1 - y, :, :, half:], y_in[unit], send.at[unit, 3], receive.at[unit, 3], y_peer
        )
        copy_x.start()
        copy_y.start()
        first_copies.append((copy_x, copy_y))

    for copy in small_plane_copies:
        copy.wait()
    small_part[...] = small_core[plane] + small_plane[0] + small_plane[1] + small_plane[2]
    small_line_copies = []
    for step, peer in enumerate(z_peers):
        index = lax.rem(z + step + 1, 4)
        copy = remote(small_part.at[index], small_line.at[step], small_send.at[4 + step], small_receive.at[4 + step], peer)
        copy.start()
        small_line_copies.append(copy)

    second_copies = []
    for unit in range(count):
        half = UNITS[unit][0] // 2
        copy_x, copy_y = first_copies[unit]
        copy_x.wait()
        for part in range(2):
            for line in range(4):
                x_in[unit][part, line] = (
                    x_in[unit][part, line].astype(F32) + core_in[unit][part, line, x, 0:half].astype(F32)
                ).astype(BF16)
        again_y = remote(
            x_in[unit].at[1 - y], late[unit].at[:, 0:half], send.at[unit, 4], receive.at[unit, 4], y_peer
        )
        again_y.start()
        copy_y.wait()
        for line in range(4):
            for side in range(2):
                y_in[unit][line, side] = (
                    y_in[unit][line, side].astype(F32) + core_in[unit][y, line, side, half:].astype(F32)
                ).astype(BF16)
        again_x = remote(
            y_in[unit].at[:, 1 - x], late[unit].at[:, half:], send.at[unit, 5], receive.at[unit, 5], x_peer
        )
        again_x.start()
        second_copies.append((again_y, again_x))

    for copy in small_line_copies:
        copy.wait()
    own = small_part[z] + small_line[0] + small_line[1] + small_line[2]
    small_out[core, plane, z] = own
    gather = []
    for step, peer in enumerate(z_peers):
        copy = remote(
            small_out.at[core, plane, z], small_out.at[core, plane, z], small_send.at[7 + step], small_receive.at[7 + step], peer
        )
        copy.start()
        gather.append(copy)

    line_copies = []
    for unit in range(count):
        half = UNITS[unit][0] // 2
        again_y, again_x = second_copies[unit]
        again_y.wait()
        again_x.wait()
        for line in range(4):
            late[unit][line, 0:half] = (
                late[unit][line, 0:half].astype(F32) + x_in[unit][y, line].astype(F32)
            ).astype(BF16)
            late[unit][line, half:] = (
                late[unit][line, half:].astype(F32) + y_in[unit][line, x].astype(F32)
            ).astype(BF16)
        copies = []
        for step, peer in enumerate(z_peers):
            copy = remote(
                late[unit].at[lax.rem(z + step + 1, 4)], line_in[unit].at[step],
                send.at[unit, 6 + step], receive.at[unit, 6 + step], peer,
            )
            copy.start()
            copies.append(copy)
        line_copies.append(copies)

    for copy in gather:
        copy.wait()
    plane_gather = []
    for step, (peer, _) in enumerate(plane_peers):
        copy = remote(
            small_out.at[core, plane], small_out.at[core, plane], small_send.at[10 + step], small_receive.at[10 + step], peer
        )
        copy.start()
        plane_gather.append(copy)
    for copy in plane_gather:
        copy.wait()
    last = remote(small_out.at[core], small_out.at[core], small_send.at[13], small_receive.at[13], core_peer)
    last.start()

    for unit in range(count):
        for copy in line_copies[unit]:
            copy.wait()
        total = late[unit][z].astype(F32)
        for step in range(3):
            total = total + line_in[unit][step].astype(F32)
        outs[unit][...] = total
    last.wait()


def reduce_small_mesh(units, small):
    count = len(UNITS)
    scratch = []
    for shape in (
        lambda r, c: (2, 4, 2, r, c),
        lambda r, c: (2, 4, r // 2, c),
        lambda r, c: (4, 2, r // 2, c),
        lambda r, c: (4, r, c),
        lambda r, c: (3, r, c),
    ):
        scratch += [pltpu.VMEM(shape(*unit), BF16) for unit in UNITS]
    scratch += [
        pltpu.VMEM((4, 4, 16, 128), F32),
        pltpu.VMEM((3, 4, 16, 128), F32),
        pltpu.VMEM((3, 16, 128), F32),
        pltpu.VMEM((4, 16, 128), F32),
        pltpu.SemaphoreType.DMA((count, 9)),
        pltpu.SemaphoreType.DMA((count, 9)),
        pltpu.SemaphoreType.DMA((14,)),
        pltpu.SemaphoreType.DMA((14,)),
    ]
    shaped = [item.reshape((4, 4, 2) + unit) for item, unit in zip(units, UNITS)]
    results = pl.pallas_call(
        reduce_kernel,
        out_shape=[jax.ShapeDtypeStruct(unit, F32) for unit in UNITS]
        + [jax.ShapeDtypeStruct((2, 4, 4, 16, 128), F32)],
        in_specs=[whole()] * (count + 1),
        out_specs=[whole()] * (count + 1),
        scratch_shapes=scratch,
        compiler_params=pltpu.CompilerParams(
            collective_id=2, has_side_effects=True, vmem_limit_bytes=VMEM_LIMIT
        ),
        name="reduce",
    )(*shaped, small.reshape(2, 4, 4, 16, 128))
    return list(results[:count]), results[count].reshape(SMALL_ROWS, 128)


def reduce_any_mesh(units, small):
    done = []
    for item in units:
        part = lax.psum_scatter(item.reshape((4, -1) + item.shape[-2:]), "seq", scatter_dimension=0, tiled=True)
        part = part.reshape(part.shape[1:])
        count = lax.axis_size("rows")
        part = part.reshape((count, -1, part.shape[-1]))
        part = lax.psum_scatter(part, "rows", scatter_dimension=0, tiled=True)
        done.append(part.reshape(part.shape[1:]).astype(F32))
    return done, lax.psum(small, ("rows", "seq"))


def whole():
    return pl.BlockSpec(memory_space=pltpu.VMEM)


def scalars():
    return pl.BlockSpec(memory_space=pltpu.SMEM)


def on_device(layer_input, first_gain, first_shift, input_weight, query_bias, value_bias, bias_table, output_weight, output_bias, attention_scale, second_gain, second_shift, up_weight, up_bias, down_weight, down_bias, feed_scale, upstream, grid_heights, grid_widths, packing_order):
    parts = lax.axis_size("seq")
    slots = layer_input.shape[1]
    hidden_units = up_weight.shape[1]

    def line(item):
        return item.reshape(1, -1)

    def shape(*dims, dtype=F32):
        return jax.ShapeDtypeStruct(dims, dtype)

    table = bias_table.reshape(SPAN, SPAN, HEADS)
    reversed_table = jnp.pad(
        jnp.transpose(table[:, ::-1, :], (0, 2, 1)).astype(F32),
        ((0, 0), (0, 16 - HEADS), (0, 128 - SPAN)),
    )
    near_table = table[GRID - 3 : GRID + 2, GRID - 3 : GRID + 2].reshape(25, HEADS).astype(F32)

    tokens, own_upstream = pl.pallas_call(
        functools.partial(spread_kernel, parts),
        out_shape=[shape(SLOTS, MODEL, dtype=BF16)] * 2,
        in_specs=[whole()] * 2,
        out_specs=[whole()] * 2,
        scratch_shapes=[
            pltpu.SemaphoreType.DMA((2, parts - 1)),
            pltpu.SemaphoreType.DMA((2, parts - 1)),
            pltpu.SemaphoreType.DMA((2,)),
        ],
        compiler_params=pltpu.CompilerParams(collective_id=0, has_side_effects=True, vmem_limit_bytes=VMEM_LIMIT),
        name="spread",
    )(layer_input, upstream)

    full = (SLOTS, MODEL)
    first, query, keys, values, chance, attended, inverse, branch, middle, second, attended_low, picks, query_codes, key_code = pl.pallas_call(
        forward_kernel,
        out_shape=[shape(*full, dtype=BF16)] * 4
        + [shape(HEADS, SLOTS, PADDED, dtype=BF16)]
        + [shape(*full)] * 4
        + [shape(*full, dtype=BF16)] * 2
        + [shape(SLOTS, 128, dtype=BF16), shape(2, SLOTS, 128), shape(8, PADDED)],
        in_specs=[scalars()] * 4 + [whole()] * 12,
        out_specs=[whole()] * 14,
        scratch_shapes=[
            pltpu.VMEM((HEADS, 2, 8, WIDE), F32),
            pltpu.VMEM((HEADS, 128, 128), BF16),
            pltpu.VMEM((SLOTS, SLOTS), F32),
            pltpu.VMEM((STRIP, WIDE), F32),
            pltpu.VMEM((STRIP, WIDE), F32),
        ],
        compiler_params=pltpu.CompilerParams(vmem_limit_bytes=VMEM_LIMIT),
        name="forward",
    )(
        grid_heights, grid_widths, packing_order, near_table, reversed_table, tokens,
        line(first_gain), line(first_shift), input_weight, line(query_bias), line(value_bias),
        output_weight, line(output_bias), line(attention_scale), line(second_gain), line(second_shift),
    )

    tiles = hidden_units // MODEL

    def fixed(*dims):
        return pl.BlockSpec(dims, lambda tile: (0,) * len(dims))

    output, second_change, up_unit, down_unit, up_sum, feed_sums = pl.pallas_call(
        feed_kernel,
        grid=(tiles,),
        out_shape=[
            shape(*full, dtype=BF16),
            shape(*full),
            shape(4, MODEL, MODEL, dtype=BF16),
            shape(4, 8, 192, 384, dtype=BF16),
            shape(tiles, 8, MODEL),
            shape(2, 8, MODEL),
        ],
        in_specs=[
            fixed(*full),
            fixed(*full),
            fixed(*full),
            pl.BlockSpec((MODEL, MODEL), lambda tile: (0, tile)),
            pl.BlockSpec((1, MODEL), lambda tile: (0, tile)),
            pl.BlockSpec((MODEL, MODEL), lambda tile: (tile, 0)),
            fixed(1, MODEL),
            fixed(1, MODEL),
        ],
        out_specs=[
            fixed(*full),
            fixed(*full),
            pl.BlockSpec((1, MODEL, MODEL), lambda tile: (tile, 0, 0)),
            pl.BlockSpec((4, 2, 192, 384), lambda tile: (0, tile, 0, 0)),
            pl.BlockSpec((1, 8, MODEL), lambda tile: (tile, 0, 0)),
            fixed(2, 8, MODEL),
        ],
        scratch_shapes=[
            pltpu.VMEM(full, BF16),
            pltpu.VMEM(full, F32),
            pltpu.VMEM(full, BF16),
            pltpu.VMEM(full, BF16),
            pltpu.VMEM(full, F32),
            pltpu.VMEM(full, F32),
        ],
        compiler_params=pltpu.CompilerParams(vmem_limit_bytes=VMEM_LIMIT),
        name="feed",
    )(second, middle, own_upstream, up_weight, line(up_bias), down_weight, line(down_bias), line(feed_scale))

    gradient, input_unit, output_unit, table_sum, sums = pl.pallas_call(
        backward_kernel,
        out_shape=[
            shape(*full, dtype=BF16),
            shape(4, MODEL, 576, dtype=BF16),
            shape(4, MODEL, 192, dtype=BF16),
            shape(SPAN, 16, 128),
            shape(8, 8, MODEL),
        ],
        in_specs=[scalars()] * 3 + [whole()] * 21,
        out_specs=[whole()] * 5,
        scratch_shapes=[
            pltpu.VMEM(full, F32),
            pltpu.VMEM(full, BF16),
            pltpu.VMEM(full, BF16),
            pltpu.VMEM((SLOTS, 3 * MODEL), BF16),
            pltpu.VMEM((HEADS, 2, 8, WIDE), F32),
            pltpu.VMEM((HEADS, 128, 128), F32),
            pltpu.VMEM((SLOTS, PADDED), F32),
            pltpu.VMEM((SLOTS, PADDED), BF16),
            pltpu.VMEM(full, F32),
        ],
        input_output_aliases={},
        compiler_params=pltpu.CompilerParams(vmem_limit_bytes=VMEM_LIMIT),
        name="backward",
    )(
        grid_heights, grid_widths, packing_order, tokens, own_upstream, middle, branch, second_change,
        attended, attended_low, inverse, first, query, keys, values, chance, picks, query_codes, key_code,
        input_weight, output_weight, line(attention_scale), line(second_gain), line(first_gain),
    )

    own_output, own_gradient = pl.pallas_call(
        functools.partial(gather_kernel, parts),
        out_shape=[shape(parts, slots, MODEL, dtype=BF16)] * 2,
        in_specs=[whole()] * 2,
        out_specs=[whole()] * 2,
        scratch_shapes=[
            pltpu.SemaphoreType.DMA((2, parts - 1)),
            pltpu.SemaphoreType.DMA((2, parts - 1)),
            pltpu.SemaphoreType.DMA((2,)),
        ],
        compiler_params=pltpu.CompilerParams(collective_id=1, has_side_effects=True, vmem_limit_bytes=VMEM_LIMIT),
        name="gather",
    )(output, gradient)

    vectors = jnp.concatenate([jnp.sum(sums, 1), jnp.sum(feed_sums, 1), jnp.sum(up_sum, 1)], 0)
    table_flat = jnp.concatenate([table_sum[:, :HEADS, :64], jnp.zeros((1, HEADS, 64), F32)], 0)
    table_flat = table_flat.reshape(-1, 128)
    vector_flat = vectors.reshape(-1, 128)
    used = table_flat.shape[0] + vector_flat.shape[0]
    small = jnp.concatenate([table_flat, vector_flat, jnp.zeros((SMALL_ROWS - used, 128), F32)], 0)
    units = (input_unit, output_unit, up_unit, down_unit)
    if (lax.axis_size("rows"), parts) == (8, 4):
        done, small = reduce_small_mesh(units, small)
        done[3] = done[3].T
    else:
        done, small = reduce_any_mesh(units[:3] + (jnp.transpose(down_unit, (0, 1, 3, 2)),), small)
    table_done = small[: table_flat.shape[0]].reshape(SPAN + 1, HEADS, 64)[:SPAN, :, :SPAN]
    table_done = jnp.transpose(table_done[:, :, ::-1], (0, 2, 1)).reshape(-1, HEADS)
    vectors = small[table_flat.shape[0] : used].reshape(-1, MODEL)
    return (
        own_output,
        own_gradient.astype(F32),
        vectors[0],
        vectors[1],
        done[0],
        vectors[2],
        vectors[3],
        table_done,
        done[1],
        vectors[4],
        vectors[5],
        vectors[6],
        vectors[7],
        done[2],
        vectors[10:].reshape(-1),
        done[3],
        vectors[9],
        vectors[8],
    )


def solution(mesh):
    split = P("rows", "seq", None)
    lines = P("rows", None)
    block = P("rows", "seq")
    in_specs = (split,) + (P(),) * 16 + (split, lines, lines, lines)
    out_specs = (split, split, P(), P(), block, P(), P(), P(), block, P(), P(), P(), P(), block, P(), block, P(), P())
    return jax.shard_map(on_device, mesh=mesh, in_specs=in_specs, out_specs=out_specs, check_vma=False)
```

time: 1300 us -> 316 us (0.24)
  matrix products: 495 us -> 0 us
  local copies, waits for them, and re-layouts: 385 us -> 17.5 us
  Pallas kernels: 0 us -> 291 us
  waiting for transfers between devices: 229 us -> 0 us
  other arithmetic: 120 us -> 5.31 us
  blocking collectives: 41.9 us -> 0 us
  between operations: 17.3 us -> 0.94 us
    dot_general x48 -> x0, matrix products: 495 us -> none  [the longest x46 328 us: product(): return jnp.einsum(form, left, right, preferred_element_type=jnp.float32)]
    pallas_call x0 -> x6, Pallas kernels: none -> 291 us  [the longest x1 104 us: reduce_small_mesh(): pl.pallas_call(reduce_kernel, out_shape=[jax.ShapeDtypeStruct(unit, F32)...]
    reshape x12 -> x18, local copies, waits for them, and re-layouts: 155 us -> 9.06 us  [the longest x11 6.42 us: line(): return item.reshape(1, -1)]
    convert_element_type x7 -> x1, local copies, waits for them, and re-layouts: 129 us -> 0.62 us  [on_device(): table[GRID - 3:GRID + 2, GRID - 3:GRID + 2].reshape(25, HEADS).astype(F32)]
    ppermute x7 -> x0, waiting for transfers between devices: 123 us -> none  [shifted(): return lax.ppermute(value, axis, pairs)]
    convert_element_type x26 -> x1, other arithmetic: 71.7 us -> 2.61 us  [on_device(): own_gradient.astype(F32)]
    psum x1 -> x0, waiting for transfers between devices: 60.4 us -> none  [on_device(): lax.psum((first_gain_gradient, first_shift_gradient, query_bias_gradient,...]
    reduce_scatter x5 -> x0, waiting for transfers between devices: 44.9 us -> none  [the longest x1 44.9 us: on_device(): lax.psum_scatter(weights_local[0], 'rows', scatter_dimension=0, tiled=True)]
  transfers between devices with their start and end apart: 16 -> 0, of which waited for: 8 -> 0; matrix products, arithmetic and copies ran while one was open for 66% -> 0% of each run, Pallas kernels for 0% -> 0%
where the time goes in v1:
time: 316 us; the launch traced here: 315 us
  Pallas kernels  291 us (92%)
  local copies, waits for them, and re-layouts  17.5 us (6%)
  other arithmetic  5.31 us (2%)
    pallas_call x1, Pallas kernels, reduce_small_mesh(): pl.pallas_call(reduce_kernel, out_shape=[jax.ShapeDtypeStruct(unit, F32)...  104 us
    pallas_call x1, Pallas kernels, on_device(): pl.pallas_call(backward_kernel, out_shape=[shape(*full, dtype=BF16), shap...  57.4 us
    pallas_call x1, Pallas kernels, on_device(): pl.pallas_call(forward_kernel, out_shape=[shape(*full, dtype=BF16)] * 4 +...  46.5 us
    pallas_call x1, Pallas kernels, on_device(): pl.pallas_call(feed_kernel, grid=(tiles,), out_shape=[shape(*full, dtype=...  35.6 us
    pallas_call x1, Pallas kernels, on_device(): pl.pallas_call(functools.partial(spread_kernel, parts), out_shape=[shape(...  23.9 us
    pallas_call x1, Pallas kernels, on_device(): pl.pallas_call(functools.partial(gather_kernel, parts), out_shape=[shape(...  23.8 us
    reshape x11, local copies, waits for them, and re-layouts, line(): return item.reshape(1, -1)  6.42 us

profile of v1, /device:TPU:8, one launch (start us, length us, event | category | flops | bytes accessed | tf_op | source)
XLA Modules:
  0.0 314.6 jit_solution(2774548996378660551)
XLA Ops:
  0.7 0.0 copy-start.6
  0.7 0.0 copy-start.9
  0.7 0.0 copy-start.10
  0.7 0.0 copy-start.11
  0.7 0.0 copy-start.12
  0.7 0.0 copy-start.13
  0.7 0.0 copy-start.14
  0.7 0.0 copy-start.15
  0.7 0.0 copy-start.16
  0.7 23.9 %spread.1 = (bf16[576,768]{1,0:T(8,128)(2,1)}, bf16[576,768]{1,0:T(8,128)(2,1)}) custom-call(bf16[4,144,768]{2,1,0:T(8,128)(2,1)} %tokens.1, bf16[4,144,768]{2,1,0:T(8,128)(2,1)} %upstream.1), custom_call_target="tpu_custom_call" | custom-call | tf_op jit(solution)/shard_map/spread/pallas_call | solution.py:817
  24.6 0.0 copy-done.6
  24.6 0.2 reshape.134
  24.9 0.1 rev.6
  25.0 0.8 pad_convert_fusion.reversed_table
  25.8 0.1 slice.83
  25.9 0.1 copy.48
  26.1 0.6 reshape.157.near_table
  26.7 0.0 copy-done.9
  26.7 0.6 reshape.135.first_gain
  27.3 0.0 copy-done.10
  27.3 0.6 reshape.140.attention_scale
  27.8 0.0 copy-done.11
  27.9 0.6 reshape.141.second_gain
  28.4 0.0 copy-done.12
  28.4 0.6 reshape.136.first_shift
  29.0 0.0 copy-done.13
  29.0 0.6 reshape.137.query_bias
  29.6 0.0 copy-done.14
  29.6 0.6 reshape.138.value_bias
  30.2 0.0 copy-done.15
  30.2 0.6 reshape.139.output_bias
  30.8 0.0 copy-done.16
  30.8 0.6 reshape.142.second_shift
  31.4 46.5 %forward.1 = (bf16[576,768]{1,0:T(8,128)(2,1)}, bf16[576,768]{1,0:T(8,128)(2,1)}, bf16[576,768]{1,0:T(8,128)(2,1)}, bf16[576,768]{1,0:T(8,128)(2,1)}, bf16[12,57...) custom-call(s32[4,4]{1,0:T(4,128)} %heights.3, ...), custom_call_target="tpu_custom_call" | custom-call | tf_op jit(solution)/shard_map/forward/pallas_call | solution.py:832
  77.9 0.0 copy-done.8
  77.9 0.6 reshape.143.up_bias
  78.5 0.0 copy-done.17
  78.5 0.6 reshape.144.down_bias
  79.1 0.0 copy-done.18
  79.1 0.6 reshape.145.feed_scale
  79.6 35.6 %feed.1 = (bf16[576,768]{1,0:T(8,128)(2,1)}, f32[576,768]{1,0:T(8,128)}, bf16[4,768,768]{2,1,0:T(8,128)(2,1)}, bf16[4,8,192,384]{3,2,1,0:T(8,128)(2,1)}, f32[4,8,768]{2,1,0:T(8,128)}, /*index=5*/f32[2,8,768]{2,1,0:T(8,128)}) custom-call(bf16[576,768]{1,0:T(8,128)(2,1)} %get-tuple-element.53.second, f32[576,768]{1,0:T(8,128)} %get-tuple-element.54.middle, ...), custom_call_target="tpu_custom_call" | custom-call | tf_op jit(solution)/shard_map/feed/pallas_call | solution.py:861
  115.2 0.0 copy-start.7
  115.3 57.4 %backward.1 = (bf16[576,768]{1,0:T(8,128)(2,1)}, bf16[4,768,576]{2,1,0:T(8,128)(2,1)}, bf16[4,768,192]{2,1,0:T(8,128)(2,1)}, f32[47,16,128]{2,1,0:T(8,128)}, f32[8,8,768]{2,1,0:T(8,128)}) custom-call(s32[4,4]{1,0:T(4,128)} %heights.3, s32[4,4]{1,0:T(4,128)} %widths.3, s32[4,4]{1,0:T(4,128)} %order.3, bf16[576,768]{1,0:T(8,128)(2,1)} %get-tuple-element.52.tokens, ...), custom_call_target="tpu_custom_call" | custom-call | tf_op jit(solution)/shard_map/backward/pallas_call | solution.py:902
  172.7 1.0 reduce_sum.27
  173.7 0.0 copy-done.5
  173.8 1.0 concatenate.9
  174.8 0.1 reshape.150
  175.0 0.1 pad.11.clone
  175.0 0.8 maximum_maximum_fusion
  175.9 103.6 %reduce.1 = (f32[96,576]{1,0:T(8,128)}, f32[96,192]{1,0:T(8,128)}, f32[96,768]{1,0:T(8,128)}, f32[192,384]{1,0:T(8,128)}, f32[2,4,4,16,128]{4,3,2,1,0:T(8,128)}) custom-call(bf16[4,4,2,96,576]{4,3,2,1,0:T(8,128)(2,1)} %bitcast.38, bf16[4,4,2,96,192]{4,3,2,1,0:T(8,128)(2,1)} %bitcast.39, bf16[4,4,2,96,768]{4,3,2,1,0:T(8,128)(2,1)} %bitcast.36, ...), custom_call_target="tpu_custom_call" | custom-call | tf_op jit(solution)/shard_map/reduce/pallas_call | solution.py:764
  279.5 0.9 slice.88
  280.4 0.1 reshape.154
  280.6 0.2 rev.7
  280.7 0.1 copy.47
  280.8 0.8 reshape.155
  281.7 1.4 slice_bitcast_fusion.1
  283.1 1.3 slice_bitcast_fusion
  284.4 23.8 %gather.1 = (bf16[4,144,768]{2,1,0:T(8,128)(2,1)}, bf16[4,144,768]{2,1,0:T(8,128)(2,1)}) custom-call(bf16[576,768]{1,0:T(8,128)(2,1)} %get-tuple-element.56.output, bf16[576,768]{1,0:T(8,128)(2,1)} %get-tuple-element.70.gradient), custom_call_target="tpu_custom_call" | custom-call | tf_op jit(solution)/shard_map/gather/pallas_call | solution.py:933
  308.3 2.6 convert_element_type.17
  310.9 0.9 copy.54
  311.8 0.7 copy.55
  312.5 0.6 copy.56
  313.1 0.7 copy.57
  313.9 0.7 copy.58
  (22 shorter events, 0.2 us)
Async XLA Ops:
  0.7 24.0 %copy-start.6 = (bf16[2209,12]{0,1:T(8,128)(2,1)S(1)}, bf16[2209,12]{0,1:T(8,128)(2,1)}, u32[]{:S(2)}) copy-start(bf16[2209,12]{0,1:T(8,128)(2,1)} %param.27) | copy-start | bytes 159052
  0.7 26.0 %copy-start.9 = (bf16[768]{0:T(1024)(128)(2,1)S(1)}, bf16[768]{0:T(1024)(128)(2,1)}, u32[]{:S(2)}) copy-start(bf16[768]{0:T(1024)(128)(2,1)} %param.22) | copy-start | bytes 4612
  0.7 26.6 %copy-start.10 = (bf16[768]{0:T(1024)(128)(2,1)S(1)}, bf16[768]{0:T(1024)(128)(2,1)}, u32[]{:S(2)}) copy-start(bf16[768]{0:T(1024)(128)(2,1)} %param.30) | copy-start | bytes 4612
  0.7 27.2 %copy-start.11 = (bf16[768]{0:T(1024)(128)(2,1)S(1)}, bf16[768]{0:T(1024)(128)(2,1)}, u32[]{:S(2)}) copy-start(bf16[768]{0:T(1024)(128)(2,1)} %param.31) | copy-start | bytes 4612
  0.7 27.7 %copy-start.12 = (bf16[768]{0:T(1024)(128)(2,1)S(1)}, bf16[768]{0:T(1024)(128)(2,1)}, u32[]{:S(2)}) copy-start(bf16[768]{0:T(1024)(128)(2,1)} %param.23) | copy-start | bytes 4612
  0.7 28.3 %copy-start.13 = (bf16[768]{0:T(1024)(128)(2,1)S(1)}, bf16[768]{0:T(1024)(128)(2,1)}, u32[]{:S(2)}) copy-start(bf16[768]{0:T(1024)(128)(2,1)} %param.25) | copy-start | bytes 4612
  0.7 28.9 %copy-start.14 = (bf16[768]{0:T(1024)(128)(2,1)S(1)}, bf16[768]{0:T(1024)(128)(2,1)}, u32[]{:S(2)}) copy-start(bf16[768]{0:T(1024)(128)(2,1)} %param.26) | copy-start | bytes 4612
  0.7 29.5 %copy-start.15 = (bf16[768]{0:T(1024)(128)(2,1)S(1)}, bf16[768]{0:T(1024)(128)(2,1)}, u32[]{:S(2)}) copy-start(bf16[768]{0:T(1024)(128)(2,1)} %param.29) | copy-start | bytes 4612
  0.7 30.0 %copy-start.16 = (bf16[768]{0:T(1024)(128)(2,1)S(1)}, bf16[768]{0:T(1024)(128)(2,1)}, u32[]{:S(2)}) copy-start(bf16[768]{0:T(1024)(128)(2,1)} %param.32) | copy-start | bytes 4612
  31.4 46.5 %copy-start.8 = (bf16[3072]{0:T(1024)(128)(2,1)S(1)}, bf16[3072]{0:T(1024)(128)(2,1)}, u32[]{:S(2)}) copy-start(bf16[3072]{0:T(1024)(128)(2,1)} %param.34) | copy-start | bytes 18436
  31.4 47.1 %copy-start.17 = (bf16[768]{0:T(1024)(128)(2,1)S(1)}, bf16[768]{0:T(1024)(128)(2,1)}, u32[]{:S(2)}) copy-start(bf16[768]{0:T(1024)(128)(2,1)} %param.36) | copy-start | bytes 4612
  31.4 47.7 %copy-start.18 = (bf16[768]{0:T(1024)(128)(2,1)S(1)}, bf16[768]{0:T(1024)(128)(2,1)}, u32[]{:S(2)}) copy-start(bf16[768]{0:T(1024)(128)(2,1)} %param.37) | copy-start | bytes 4612
  115.2 58.4 %copy-start.5 = (f32[4,8,768]{2,1,0:T(8,128)S(1)}, f32[4,8,768]{2,1,0:T(8,128)}, u32[]{:S(2)}) copy-start(f32[4,8,768]{2,1,0:T(8,128)} %get-tuple-element.80) | copy-start | bytes 294916
  115.2 58.5 %copy-start.7 = (f32[2,8,768]{2,1,0:T(8,128)S(1)}, f32[2,8,768]{2,1,0:T(8,128)}, u32[]{:S(2)}) copy-start(f32[2,8,768]{2,1,0:T(8,128)} %get-tuple-element.79) | copy-start | bytes 147460
  308.2 2.6 copy-start
  308.2 3.5 %copy-start.3 = (f32[96,576]{1,0:T(8,128)S(1)}, f32[96,576]{1,0:T(8,128)}, u32[]{:S(2)}) copy-start(f32[96,576]{1,0:T(8,128)} %get-tuple-element.118) | copy-start | bytes 663556
  310.9 1.6 copy-start.4
  310.9 2.3 copy-start.2
  310.9 3.0 copy-start.1
